TPU v7x, 32 devices: a whole 2x2x4 slice. The times are simulated.
32 devices in a mesh: space: 16 (over z, x, core), mode: 2 (over y).
Axes of the slice: x: 2, y: 2, z: 4, core: 2. Of those that a mesh axis runs over, the one named last changes fastest.
Arguments:
- state: float32 [858, 4096], P(None, ('space', 'mode')), may hold values from -6 to 6
- tensor: bfloat16 [16, 286, 858], P('mode'), may hold values from -0.01171875 to 0.01171875
- table: int32 [286, 3], replicated, may hold values from 0 to 10, as said below
- thermal: float32 [3], replicated, may hold values from 0.5 to 2
- output_mode_row: int32 [16], replicated, may hold values from 0 to 857, as said below
Outputs:
- updated: float32 [858, 4096], P(None, ('space', 'mode'))
- collision: float32 [16, 4096], P('mode', 'space')
Inputs may be any that keep to these rules, and one draw needn't show every extreme that they name: `table`: each row holds the three indices of one multi-index of total degree at most 10; every such multi-index is in exactly one row. `output_mode_row`: all entries are different.
All inputs are finite; a program needn't handle non-finite values.
Results may differ from a plain program's by a relative error of at most 0.004.
Values may be sent and summed in bfloat16 or wider, within the bound.
No kernel may reach another device: no remote copies, remote signals or barrier semaphores. Data moves between devices by JAX's collectives and lax.ppermute only.
A program may use at most 64 MiB of HBM per device.

v0:
```python
import jax
import jax.numpy as jnp
from jax import lax
from jax.sharding import PartitionSpec as P

CLASSES = 3
MODES = 286


wave_bound = 5.2
courant = 0.09
collision_update = 0.1


def extended_2(x, sides, width):
    for axis, dim in sides:
        size, length = (lax.axis_size(axis), x.shape[dim])
        up = [(i, (i + 1) % size) for i in range(size)]
        down = [(j, i) for i, j in up]
        last = lax.slice_in_dim(x, length - width, length, axis=dim)
        first = lax.slice_in_dim(x, 0, width, axis=dim)
        before = lax.ppermute(last, axis, up)
        after = lax.ppermute(first, axis, down)
        x = jnp.concatenate([before, x, after], axis=dim)
    return x


def advection_matrix(table):
    codes = table[:, 0] * 144 + table[:, 1] * 12 + table[:, 2]
    along = table[:, 0].astype(jnp.float32)
    lower = (codes[None, :] == codes[:, None] - 144).astype(jnp.float32)
    higher = (codes[None, :] == codes[:, None] + 144).astype(jnp.float32)
    return jnp.sqrt(along)[:, None] * lower + jnp.sqrt(along + 1.0)[:, None] * higher


def upwind_transport(extended, state, matrix, thermal):
    blocks = extended.reshape(CLASSES, MODES, -1)
    state_after_collision = jnp.einsum(
        "ab,cbx->cax", matrix, blocks, precision=lax.Precision.HIGHEST
    )
    speed = thermal[:, None, None]
    flux = 0.5 * speed * (
        state_after_collision[:, :, :-1] + state_after_collision[:, :, 1:]
    ) - 0.5 * wave_bound * speed * (blocks[:, :, 1:] - blocks[:, :, :-1])
    change = (flux[:, :, 1:] - flux[:, :, :-1]).reshape(CLASSES * MODES, -1)
    return state - courant * change


def shards(state, tensor, table, thermal, output_mode_row):
    per_device = tensor.shape[0]
    own_modes = lax.dynamic_slice_in_dim(
        output_mode_row, lax.axis_index("mode") * per_device, per_device
    )
    mode_selector = ((own_modes // MODES)[:, None] == jnp.arange(CLASSES)[None, :]).astype(
        jnp.float32
    )
    flat = tensor.reshape(per_device * MODES, CLASSES * MODES)
    matrix = advection_matrix(table)
    slab = lax.all_gather(state, "mode", axis=1, tiled=True)
    piece = slab.astype(jnp.bfloat16)
    width = piece.shape[1]
    product = jnp.dot(flat, piece, preferred_element_type=jnp.float32).reshape(
        per_device, MODES, width
    )
    first = jnp.einsum(
        "oc,cix->oix", mode_selector, piece.reshape(CLASSES, MODES, width).astype(jnp.float32)
    )
    collision = jnp.sum(first * product, axis=1)
    extended_slab = extended_2(slab, (("space", 1),), 1)
    columns = state.shape[1]
    extended = lax.dynamic_slice_in_dim(
        extended_slab, lax.axis_index("mode") * columns, columns + 2, 1
    )
    advected_state = upwind_transport(extended, state, matrix, thermal)
    own_terms = lax.all_to_all(
        collision.astype(jnp.bfloat16), "mode", split_axis=1, concat_axis=0, tiled=True
    ).astype(collision.dtype)
    placing = (jnp.arange(CLASSES * MODES)[:, None] == output_mode_row[None, :]).astype(jnp.float32)
    collision_increment = jnp.dot(
        placing, own_terms, precision=lax.Precision.HIGHEST, preferred_element_type=jnp.float32
    )
    updated = advected_state + collision_update * collision_increment
    return (updated, collision)


def solution(mesh):
    in_specs = (P(None, ("space", "mode")), P("mode", None, None), P(), P(), P())
    out_specs = (P(None, ("space", "mode")), P("mode", "space"))
    return jax.shard_map(shards, mesh=mesh, in_specs=in_specs, out_specs=out_specs, check_vma=False)
```

profile of v0, /device:TPU:0, one launch (start us, length us, event | category | flops | bytes accessed | tf_op | source)
XLA Modules:
  0.0 39.9 jit_solution(2738741793877382780)
XLA Ops:
  0.6 14.1 %all_gather.3 = f32[858,256]{1,0:T(8,128)S(1)} all-gather(f32[858,128]{1,0:T(8,128)} %param.5), channel_id=1, replica_groups=mesh['space'=16,'mode'=2] {'mode'}, dimensions={1}, use_global_device_ids=true | all-gather | bytes 1317888 | tf_op jit(solution)/shard_map/all_gather | solution.py:59
  14.7 1.0 %fusion.28 = (f32[858,1]{1,0:T(8,128)}, f32[858,1]{1,0:T(8,128)}) fusion(f32[858,256]{1,0:T(8,128)S(1)} %all_gather.3), kind=kLoop, calls=%fused_computation.46 | loop fusion | bytes 13728 | tf_op jit(solution)/shard_map/slice | solution.py:21
  15.7 0.0 collective-permute-start
  15.7 4.4 %collective-permute-start.1 = (f32[858,1]{1,0:T(8,128)}, f32[858,1]{1,0:T(8,128)}, u32[]{:S(2)}, u32[]{:S(2)}) collective-permute-start(f32[858,1]{1,0:T(8,128)} %get-tuple-element.9), channel_id=1, source_target_pairs={{2,0},{4,2},{6,4},{8,6},{10,8},{12,10},{14,12},{16,14},{18,16},{20... | collective-permute-start | bytes 10304 | tf_op jit(solution)/shard_map/ppermute | solution.py:23
  20.2 0.0 copy-start
  20.2 0.8 %copy-done = bf16[858,256]{1,0:T(8,128)(2,1)} copy-done((bf16[858,256]{1,0:T(8,128)(2,1)}, bf16[858,256]{1,0:T(8,128)(2,1)S(1)}, u32[]{:S(2)}) %copy-start) | copy-done | bytes 439320
  21.0 0.9 %reshape.53 = bf16[3,286,256]{2,1,0:T(8,128)(2,1)} reshape(bf16[858,256]{1,0:T(8,128)(2,1)S(1)} %convert_element_type.22) | data formatting | bytes 878592 | tf_op jit(solution)/shard_map/reshape | solution.py:66
  21.9 3.6 %fusion.7 = f32[8,286,256]{2,0,1:T(8,128)S(1)} fusion(bf16[8,286,858]{2,0,1:T(8,128)(2,1)} %param.6, bf16[858,256]{1,0:T(8,128)(2,1)} %copy-done), kind=kOutput, calls=%fused_computation.15 | convolution fusion | flops 1005109248 | bytes 6708416 | tf_op jit(solution)/shard_map/dot_general | solution.py:62
  25.5 0.0 copy-start.3
  25.5 0.0 copy-start.5
  25.6 0.1 and_select_fusion
  25.7 1.6 %multiply_reduce_fusion = f32[8,256]{1,0:T(8,128)S(1)} fusion(f32[8,286,256]{2,0,1:T(8,128)S(1)} %fusion.7, bf16[3,286,256]{2,1,0:T(8,128)(2,1)} %reshape.53, s32[8]{0:T(128)S(1)} %and_select_fusion), kind=kOutput, calls=%fused_computation | convolution fusion | flops 4683800 | bytes 2790432 | tf_op jit(solution)/shard_map/oc,cix->oix/dot_general | solution.py:65
  27.3 0.0 copy-start.2
  27.3 0.6 %convert_bitcast_fusion = bf16[8,2,128]{2,0,1:T(8,128)(2,1)} fusion(f32[8,256]{1,0:T(8,128)S(1)} %multiply_reduce_fusion), kind=kLoop, calls=%fused_computation.32 | loop fusion | flops 2048 | bytes 12288 | tf_op jit(solution)/shard_map/convert_element_type | solution.py:76
  27.9 3.2 %all-to-all-start = ((bf16[8,2,128]{2,0,1:T(8,128)(2,1)}), bf16[8,2,128]{2,0,1:T(8,128)(2,1)S(1)}, u32[]{:S(2)}, u32[]{:S(2)}) async-start(bf16[8,2,128]{2,0,1:T(8,128)(2,1)} %convert_bitcast_fusion), calls=%async_computation | async-start | bytes 8192 | tf_op jit(solution)/shard_map/all_to_all | solution.py:75
  31.1 0.0 copy-done.5
  31.2 0.0 collective-permute-done
  31.2 0.0 collective-permute-done.1
  31.2 1.8 %fusion.2 = f32[858,130]{1,0:T(8,128)S(1)} fusion(s32[]{:T(128)S(6)} %select_n.11, f32[858,1]{1,0:T(8,128)} %collective-permute-done, f32[858,256]{1,0:T(8,128)S(1)} %all_gather.3, f32[858,1]{1,0:T(8,128)} %collective-permute-done.1), kind=kLoop, calls=%fused_computation.8 | loop fusion | flops 223080 | bytes 1331620 | tf_op jit(solution)/shard_map/concatenate | solution.py:24
  33.1 0.1 reshape.57
  33.2 0.3 fusion.27
  33.5 0.0 copy-done.2
  33.5 0.3 copy.21
  33.8 0.3 copy.22
  34.2 3.6 %convolution_bitcast_fusion = f32[3,286,130]{1,2,0:T(8,128)S(1)} fusion(f32[3,286,130]{2,1,0:T(8,128)S(1)} %reshape.57, f32[286]{0:T(512)S(1)} %get-tuple-element.3, f32[286]{0:T(512)S(1)} %get-tuple-element.2, s32[286]{0:T(512)S(1)} %get-tuple-element.6, s32[286]{0:T(512)S(1)} %get-tuple-element.5, s32[286]{0:T(512)S(1)} %get-tuple-element.4), kind=kOutput, calls=%fused_computation.4 | convolution fusion | flops 383214272 | bytes 898040 | tf_op jit(solution)/shard_map/ab,cbx->cax/dot_general | solution.py:38
  37.7 0.2 fusion.4
  38.0 0.0 copy-start.1
  38.0 0.1 fusion.5
  38.1 0.2 copy.13
  38.3 0.0 all-to-all-done
  38.3 0.7 %copy-done.1 = f32[858,128]{1,0:T(8,128)S(1)} copy-done((f32[858,128]{1,0:T(8,128)S(1)}, f32[858,128]{1,0:T(8,128)}, u32[]{:S(2)}) %copy-start.1) | copy-done | bytes 439320
  39.0 1.0 %fusion = f32[858,128]{1,0:T(8,128)} fusion(f32[858,128]{1,0:T(8,128)S(1)} %copy-done.1, f32[858,128]{1,0:T(8,128)S(1)} %mul.113, s32[16]{0:T(128)S(1)} %copy-done.4, bf16[8,2,128]{2,0,1:T(8,128)(2,1)S(1)} %all-to-all-done), kind=kOutput, calls=%fused_computation.6 | convolution fusion | flops 3857568 | bytes 1322048 | tf_op jit(solution)/shard_map/dot_general | solution.py:79
  (8 shorter events, 0.2 us)
Async XLA Ops:
  15.7 15.5 %collective-permute-start = (f32[858,1]{1,0:T(8,128)}, f32[858,1]{1,0:T(8,128)}, u32[]{:S(2)}, u32[]{:S(2)}) collective-permute-start(f32[858,1]{1,0:T(8,128)} %get-tuple-element.10), channel_id=1, source_target_pairs={{0,2},{2,4},{4,6},{6,8},{8,10},{10,12},{12,14},{14,16},{16,18},{18... | collective-permute-start | bytes 10304 | tf_op jit(solution)/shard_map/ppermute | solution.py:22
  15.7 15.5 %collective-permute-start.1 = (f32[858,1]{1,0:T(8,128)}, f32[858,1]{1,0:T(8,128)}, u32[]{:S(2)}, u32[]{:S(2)}) collective-permute-start(f32[858,1]{1,0:T(8,128)} %get-tuple-element.9), channel_id=1, source_target_pairs={{2,0},{4,2},{6,4},{8,6},{10,8},{12,10},{14,12},{16,14},{18,16},{20... | collective-permute-start | bytes 10304 | tf_op jit(solution)/shard_map/ppermute | solution.py:23
  20.2 0.8 %copy-start = (bf16[858,256]{1,0:T(8,128)(2,1)}, bf16[858,256]{1,0:T(8,128)(2,1)S(1)}, u32[]{:S(2)}) copy-start(bf16[858,256]{1,0:T(8,128)(2,1)S(1)} %convert_element_type.22) | copy-start | bytes 1317892
  21.9 3.7 %copy-start.4 = (s32[16]{0:T(128)S(1)}, s32[16]{0:T(128)}, u32[]{:S(2)}) copy-start(s32[16]{0:T(128)} %param.9) | copy-start | bytes 196
  25.5 5.6 %copy-start.3 = (s32[286,3]{0,1:T(4,128)S(1)}, s32[286,3]{0,1:T(4,128)}, u32[]{:S(2)}) copy-start(s32[286,3]{0,1:T(4,128)} %param.7) | copy-start | bytes 10300
  25.5 5.6 %copy-start.5 = (f32[3]{0:T(128)S(1)}, f32[3]{0:T(128)}, u32[]{:S(2)}) copy-start(f32[3]{0:T(128)} %param.8) | copy-start | bytes 40
  27.3 6.2 %copy-start.2 = (f32[8,256]{1,0:T(8,128)}, f32[8,256]{1,0:T(8,128)S(1)}, u32[]{:S(2)}) copy-start(f32[8,256]{1,0:T(8,128)S(1)} %multiply_reduce_fusion) | copy-start | bytes 24580
  27.9 10.4 %all-to-all-start = ((bf16[8,2,128]{2,0,1:T(8,128)(2,1)}), bf16[8,2,128]{2,0,1:T(8,128)(2,1)S(1)}, u32[]{:S(2)}, u32[]{:S(2)}) async-start(bf16[8,2,128]{2,0,1:T(8,128)(2,1)} %convert_bitcast_fusion), calls=%async_computation | async-start | bytes 8192 | tf_op jit(solution)/shard_map/all_to_all | solution.py:75
  38.0 1.0 %copy-start.1 = (f32[858,128]{1,0:T(8,128)S(1)}, f32[858,128]{1,0:T(8,128)}, u32[]{:S(2)}) copy-start(f32[858,128]{1,0:T(8,128)} %param.5) | copy-start | bytes 1317892
where the time goes:
time: 40.2 us; the launch traced here: 39.9 us
  blocking collectives  14.1 us (35%)
  matrix products  9.8 us (24%)
  starting transfers between devices  7.65 us (19%)
  local copies, waits for them, and re-layouts  4.69 us (12%)
  other arithmetic  2.91 us (7%)
  between operations  0.83 us (2%)
    all_gather x1, blocking collectives, shards(): slab = lax.all_gather(state, 'mode', axis=1, tiled=True)  14.1 us
    ppermute x1, starting transfers between devices, extended_2(): after = lax.ppermute(first, axis, down)  4.44 us
    dot_general x1, matrix products, shards(): jnp.dot(flat, piece, preferred_element_type=jnp.float32)  3.63 us
    dot_general x1, matrix products, upwind_transport(): jnp.einsum('ab,cbx->cax', matrix, blocks, precision=lax.Precision.HIGHEST)  3.58 us
    all_to_all x1, starting transfers between devices, shards(): lax.all_to_all(collision.astype(jnp.bfloat16), 'mode', split_axis=1, conc...  3.21 us
    unnamed x14, local copies, waits for them, and re-layouts  2.13 us
    concatenate x1, other arithmetic, extended_2(): x = jnp.concatenate([before, x, after], axis=dim)  1.84 us
    dot_general x1, matrix products, shards(): jnp.einsum('oc,cix->oix', mode_selector, piece.reshape(CLASSES, MODES, wi...  1.61 us
  transfers between devices with their start and end apart: 3, of which 0 were waited for; matrix products, arithmetic and copies ran while one was open for 35% of the time, Pallas kernels for 0%

commit v1 on v0

v1 whole, which is shorter than its diff:
```python
import jax
import jax.numpy as jnp
from jax import lax
from jax.experimental import pallas as pl
from jax.experimental.pallas import tpu as pltpu
from jax.sharding import PartitionSpec as P

CLASSES = 3

wave_bound = 5.2
courant = 0.09
collision_update = 0.1

BF16 = jnp.bfloat16
F32 = jnp.float32
VMEM = pl.BlockSpec(memory_space=pltpu.VMEM)
HBM = pl.BlockSpec(memory_space=pltpu.HBM)
PARAMS = pltpu.CompilerParams(vmem_limit_bytes=16 * 2**20)


def remain(x):
    return pltpu.with_memory_space_constraint(x, pltpu.HBM)


def dot(a, b):
    return jnp.dot(a, b, preferred_element_type=F32)


def dot_general(a, b, da, db):
    return lax.dot_general(a, b, (((da,), (db,)), ((), ())), preferred_element_type=F32)


def halves(x):
    high = x.astype(BF16)
    return high, (x - high.astype(F32)).astype(BF16)


def iota(shape, axis):
    return lax.broadcasted_iota(jnp.int32, shape, axis)


def coarsen_kernel(state_hbm, coarse_ref, state_ref, sems):
    rows = state_ref.shape[0]
    cut = rows // 2 // 16 * 16
    copies = []
    for j, (start, size) in enumerate(((0, cut), (cut, rows - cut))):
        part = pl.ds(start, size)
        copies.append((part, pltpu.make_async_copy(state_hbm.at[part], state_ref.at[part], sems.at[j])))
        copies[-1][1].start()
    for part, copy in copies:
        copy.wait()
        coarse_ref[part] = state_ref[part].astype(BF16)


def coarsen(state):
    return pl.pallas_call(
        coarsen_kernel,
        in_specs=[HBM],
        out_shape=(pltpu.VMEM(state.shape, BF16), pltpu.VMEM(state.shape, F32)),
        out_specs=(VMEM,) * 2,
        scratch_shapes=[pltpu.SemaphoreType.DMA((2,))],
        compiler_params=PARAMS,
        name="coarsen",
    )(remain(state))


def steps_of(modes, terms):
    for count in range(min(32, modes), 0, -1):
        if modes % count == 0 and count * terms % 16 == 0:
            return modes // count
    return 1


def contract(tensor_ref, coarse_ref, wide_ref, class_ref, steps, ready=None):
    terms, columns = class_ref.shape
    modes = tensor_ref.shape[0] // terms
    wide_ref[...] = coarse_ref[...].astype(F32)
    count = modes // steps
    sums = [jnp.zeros((terms, columns), F32) for _ in range(CLASSES)]
    for j in range(steps):
        if ready is not None:
            ready(j)
        product = dot(tensor_ref[pl.ds(j * count * terms, count * terms)], coarse_ref[...])
        product = product.reshape(count, terms, columns)
        for c in range(CLASSES):
            first = wide_ref[pl.ds(c * modes + j * count, count)]
            sums[c] = sums[c] + jnp.sum(first[:, None, :] * product, axis=0)
    total = jnp.zeros((terms, columns), F32)
    for c in range(CLASSES):
        total = total + jnp.where(class_ref[...] == c, sums[c], 0.0)
    return total


def advection_halves(table_ref, high_ref, low_ref):
    modes = table_ref.shape[1]
    index = [table_ref[j : j + 1, :].astype(F32) for j in range(3)]
    row = iota((8, modes), 0)
    weighted = jnp.where(row == 0, 144.0 * index[0], jnp.where(row == 1, 12.0 * index[1], index[2]))
    weighted = jnp.where(row < 3, weighted, 0.0).astype(BF16)
    along = jnp.where(row == 0, index[0], 0.0).astype(BF16)
    ones = jnp.ones((8, modes), BF16)
    code_down = dot_general(weighted, ones, 0, 0)
    along_down = dot_general(along, ones, 0, 0)
    code_across = 144.0 * index[0] + 12.0 * index[1] + index[2]
    matrix = jnp.where(code_across == code_down - 144.0, jnp.sqrt(along_down), 0.0)
    matrix = matrix + jnp.where(code_across == code_down + 144.0, jnp.sqrt(along_down + 1.0), 0.0)
    high_ref[...], low_ref[...] = halves(matrix)


def own_work(hbm, coarse_ref, outs, scratch):
    tensor_hbm, table_hbm, thermal_hbm, target_hbm = hbm
    tensor_ref, own_ref, high_ref, low_ref, class_ref, here_ref, there_ref, speed_ref = outs
    wide_ref, table_ref, thermal_ref, target_ref, sems = scratch
    terms, columns = class_ref.shape
    rows, modes = coarse_ref.shape[0], high_ref.shape[0]
    outputs = target_ref.shape[0]
    pairs = (table_hbm, table_ref), (target_hbm, target_ref), (thermal_hbm, thermal_ref)
    small = [pltpu.make_async_copy(source, target, sems.at[j]) for j, (source, target) in enumerate(pairs)]
    for copy in small:
        copy.start()
    steps = sems.shape[0] - len(small)
    size = modes // steps * terms
    parts = []
    for j in range(steps):
        part = pl.ds(j * size, size)
        parts.append(pltpu.make_async_copy(tensor_hbm.at[part], tensor_ref.at[part], sems.at[len(small) + j]))
        parts[-1].start()
    for copy in small:
        copy.wait()
    first = lax.axis_index("mode") * terms
    for place_ref, start in ((here_ref, first), (there_ref, first + terms)):
        lane = iota(place_ref.shape, 1)
        target = jnp.zeros(place_ref.shape, jnp.int32)
        for j in range(place_ref.shape[1]):
            target = jnp.where(lane == j, target_ref[lax.rem(start + j, outputs)], target)
        place_ref[...] = (iota(place_ref.shape, 0) == target).astype(BF16)
    line = iota((terms, columns), 0)
    kind = jnp.zeros((terms, columns), jnp.int32)
    for j in range(terms):
        target = target_ref[first + j]
        own_class = sum((target >= c * modes).astype(jnp.int32) for c in range(1, CLASSES))
        kind = jnp.where(line == j, own_class, kind)
    class_ref[...] = kind
    line = iota(speed_ref.shape, 0)
    speed = jnp.zeros(speed_ref.shape, F32)
    for c in range(CLASSES):
        speed = jnp.where(line == c, thermal_ref[c], speed)
    speed_ref[...] = speed
    advection_halves(table_ref, high_ref, low_ref)
    own_ref[...] = contract(tensor_ref, coarse_ref, wide_ref, class_ref, steps, lambda j: parts[j].wait())


def at_seam():
    return jnp.logical_and(lax.axis_index("space") == 0, lax.axis_index("mode") == 0)


def early_kernel(coarse_ref, *refs):
    hbm, edge_ref, outs, scratch = refs[:4], refs[4], refs[5:13], refs[13:]
    columns = coarse_ref.shape[1]
    wanted = jnp.where(lax.axis_index("mode") == 0, 0, columns - 1)
    pick = (iota((edge_ref.shape[0], columns), 1) == wanted).astype(BF16)
    edge_ref[...] = dot_general(pick, coarse_ref[...], 1, 1).astype(BF16)

    @pl.when(at_seam())
    def _():
        own_work(hbm, coarse_ref, outs, scratch)


def late_kernel(coarse_ref, *refs):
    hbm, outs, scratch = refs[:4], refs[12:20], refs[20:]

    @pl.when(jnp.logical_not(at_seam()))
    def _():
        own_work(hbm, coarse_ref, outs, scratch)


def own_shapes(tensor, coarse, modes, outputs):
    rows, columns = coarse.shape
    terms = tensor.shape[0] // modes
    return (
        pltpu.VMEM(tensor.shape, BF16),
        pltpu.VMEM((terms, columns), F32),
        pltpu.VMEM((modes, modes), BF16),
        pltpu.VMEM((modes, modes), BF16),
        pltpu.VMEM((terms, columns), jnp.int32),
        pltpu.VMEM((rows, terms), BF16),
        pltpu.VMEM((rows, outputs - terms), BF16),
        pltpu.VMEM((8, columns), F32),
    )


def own_scratch(coarse, tensor, table, thermal, target):
    modes = table.shape[1]
    steps = steps_of(modes, tensor.shape[0] // modes)
    return [
        pltpu.VMEM(coarse.shape, F32),
        pltpu.VMEM(table.shape, jnp.int32),
        pltpu.SMEM(thermal.shape, F32),
        pltpu.SMEM(target.shape, jnp.int32),
        pltpu.SemaphoreType.DMA((3 + steps,)),
    ]


def early(coarse, tensor, table, thermal, target):
    shapes = own_shapes(tensor, coarse, table.shape[1], target.shape[0])
    return pl.pallas_call(
        early_kernel,
        in_specs=[VMEM] + [HBM] * 4,
        out_shape=(pltpu.VMEM((8, coarse.shape[0]), BF16),) + shapes,
        out_specs=(VMEM,) * (1 + len(shapes)),
        scratch_shapes=own_scratch(coarse, tensor, table, thermal, target),
        compiler_params=PARAMS,
        name="early_work",
    )(coarse, tensor, table, thermal, target)


def late(coarse, tensor, table, thermal, target, held):
    shapes = own_shapes(tensor, coarse, table.shape[1], target.shape[0])
    return pl.pallas_call(
        late_kernel,
        in_specs=[VMEM] + [HBM] * 4 + [VMEM] * len(held),
        out_shape=shapes,
        out_specs=(VMEM,) * len(shapes),
        scratch_shapes=own_scratch(coarse, tensor, table, thermal, target),
        input_output_aliases={5 + j: j for j in range(len(held))},
        compiler_params=PARAMS,
        name="late_work",
    )(coarse, tensor, table, thermal, target, *held)


def others_kernel(tensor_ref, coarse_ref, class_ref, collision_ref, sent_ref, wide_ref):
    terms = class_ref.shape[0]
    steps = steps_of(tensor_ref.shape[0] // terms, terms)
    total = contract(tensor_ref, coarse_ref, wide_ref, class_ref, steps)
    collision_ref[...] = total
    sent_ref[...] = total.astype(BF16)


def others_collision(tensor, coarse, class_of):
    return pl.pallas_call(
        others_kernel,
        in_specs=[VMEM] * 3,
        out_shape=(pltpu.VMEM(class_of.shape, F32), pltpu.VMEM(class_of.shape, BF16)),
        out_specs=(VMEM,) * 2,
        scratch_shapes=[pltpu.VMEM(coarse.shape, F32)],
        compiler_params=PARAMS,
        name="others_collision",
    )(tensor, coarse, class_of)


def transport_kernel(
    state_ref, high_ref, low_ref, speed_ref, ring_ref, left_ref, right_ref, own_ref, here_ref, *refs
):
    others, out_ref, collision_hbm, diff_ref, collision_ref, sem = refs[:-5], *refs[-5:]
    rows, columns = state_ref.shape
    modes = high_ref.shape[0]
    me, group = lax.axis_index("mode"), lax.axis_size("mode")
    for r, terms_ref in enumerate((own_ref, *others)):
        start = pl.multiple_of(lax.rem(me + group - r, group) * columns, columns)
        collision_ref[:, pl.ds(start, columns)] = terms_ref[...]
    copy = pltpu.make_async_copy(collision_ref, collision_hbm, sem)
    copy.start()
    state = state_ref[...]
    lane = iota((rows, columns), 1)
    ones = (iota((ring_ref.shape[0], columns), 0) == 0).astype(BF16)
    ring = dot_general(ring_ref[...], ones, 0, 0)
    left = jnp.where(me == 0, ring, pltpu.roll(left_ref[...].astype(F32), 1, 1))
    right = jnp.where(me == group - 1, ring, pltpu.roll(right_ref[...].astype(F32), columns - 1, 1))
    before = jnp.where(lane == 0, left, pltpu.roll(state, 1, 1))
    after = jnp.where(lane == columns - 1, right, pltpu.roll(state, columns - 1, 1))
    diff_ref[...] = after - before
    spread = before + after - 2.0 * state
    own_high, own_low = halves(own_ref[...])
    here = here_ref[...]
    out_ref[...] = state + collision_update * (dot(here, own_high) + dot(here, own_low))
    for c in range(CLASSES):
        part = pl.ds(c * modes, modes)
        speed = speed_ref[c : c + 1, :]
        d_high, d_low = halves(diff_ref[part])
        moved = dot(high_ref[...], d_high) + dot(high_ref[...], d_low) + dot(low_ref[...], d_high)
        diffused = (0.5 * wave_bound * courant) * spread[c * modes : (c + 1) * modes]
        out_ref[part] = out_ref[part] + speed * (diffused - (0.5 * courant) * moved)
    copy.wait()


def transport(state, high, low, speed, ring, left, right, own, here, others):
    terms, columns = own.shape
    collision = (terms, (1 + len(others)) * columns)
    return pl.pallas_call(
        transport_kernel,
        in_specs=[VMEM] * (9 + len(others)),
        out_shape=(pltpu.VMEM(state.shape, F32), jax.ShapeDtypeStruct(collision, F32)),
        out_specs=(VMEM, HBM),
        scratch_shapes=[pltpu.VMEM(state.shape, F32), pltpu.VMEM(collision, F32), pltpu.SemaphoreType.DMA],
        compiler_params=PARAMS,
        name="transport",
    )(state, high, low, speed, ring, left, right, own, here, *others)


def place_kernel(base_ref, there_ref, terms_ref, out_ref):
    out_ref[...] = base_ref[...] + collision_update * dot(there_ref[...], terms_ref[...])


def place_terms(base, there, terms):
    return pl.pallas_call(
        place_kernel,
        in_specs=[VMEM] * 3,
        out_shape=jax.ShapeDtypeStruct(base.shape, F32),
        out_specs=VMEM,
        compiler_params=PARAMS,
        name="place_terms",
    )(base, there, terms)


def shards(state, tensor, table, thermal, output_mode_row):
    rows, columns = state.shape
    terms, modes, _ = tensor.shape
    slabs, group = lax.axis_size("space"), lax.axis_size("mode")

    def shift(x, by):
        return lax.ppermute(x, "mode", [(i, (i + by) % group) for i in range(group)])

    coarse, wide = coarsen(state)
    cells = {r: shift(coarse, r) for r in range(1, group)}

    flat = jnp.transpose(tensor, (1, 0, 2)).reshape(modes * terms, rows)
    given = tuple(remain(x) for x in (flat, table.T, thermal, output_mode_row))
    edge, *held = early(coarse, *given)
    size = slabs * group
    pairs = [(s * group + group - 1, (s + 1) * group % size) for s in range(slabs)]
    ring = lax.ppermute(edge, ("space", "mode"), pairs + [(j, i) for i, j in pairs])
    held_tensor, own, high, low, class_of, here, there, speed = late(coarse, *given, held)

    returned, others = [], []
    for r in range(1, group):
        terms_of, sent = others_collision(held_tensor, cells[r], class_of)
        others.append(terms_of)
        returned.append(shift(sent, group - r))

    base, collision = transport(
        wide, high, low, speed, ring, cells[1], cells[group - 1], own, here, others
    )
    arrived = returned[0] if group == 2 else jnp.concatenate(returned)
    return place_terms(base, there, arrived), collision


def solution(mesh):
    in_specs = (P(None, ("space", "mode")), P("mode", None, None), P(), P(), P())
    out_specs = (P(None, ("space", "mode")), P("mode", "space"))
    return jax.shard_map(shards, mesh=mesh, in_specs=in_specs, out_specs=out_specs, check_vma=False)
```

time: 40.2 us -> 19.2 us (0.48)
  blocking collectives: 14.1 us -> 0 us
  Pallas kernels: 0 us -> 10.1 us
  matrix products: 9.8 us -> 0 us
  local copies, waits for them, and re-layouts: 4.69 us -> 0 us
  waiting for transfers between devices: 0.01 us -> 3.02 us
  other arithmetic: 2.91 us -> 0 us
  starting transfers between devices: 7.65 us -> 5.21 us
    all_gather x1 -> x0, blocking collectives: 14.1 us -> none  [shards(): slab = lax.all_gather(state, 'mode', axis=1, tiled=True)]
    pallas_call x0 -> x6, Pallas kernels: none -> 10.1 us  [the longest x1 4.92 us: early(): pl.pallas_call(early_kernel, in_specs=[VMEM] + [HBM] * 4, out_shape=(pltp...]
    dot_general x4 -> x0, matrix products: 9.8 us -> none  [the longest x1 3.63 us: shards(): jnp.dot(flat, piece, preferred_element_type=jnp.float32)]
    all_to_all x1 -> x0, starting transfers between devices: 3.21 us -> none  [shards(): lax.all_to_all(collision.astype(jnp.bfloat16), 'mode', split_axis=1, conc...]
    ppermute x2 -> x3, waiting for transfers between devices: 0.01 us -> 3.02 us  [the longest x1 2.75 us: shards(): lax.ppermute(edge, ('space', 'mode'), pairs + [(j, i) for i, j in pairs])]
    unnamed x14 -> x0, local copies, waits for them, and re-layouts: 2.13 us -> none
    concatenate x1 -> x0, other arithmetic: 1.84 us -> none  [extended_2(): x = jnp.concatenate([before, x, after], axis=dim)]
    slice x2 -> x0, local copies, waits for them, and re-layouts: 1.35 us -> none  [the longest x1 1.04 us: extended_2(): first = lax.slice_in_dim(x, 0, width, axis=dim)]
  transfers between devices with their start and end apart: 3 -> 3, of which waited for: 0 -> 2; matrix products, arithmetic and copies ran while one was open for 35% -> 0% of each run, Pallas kernels for 0% -> 43%
where the time goes in v1:
time: 19.2 us; the launch traced here: 19 us
  Pallas kernels  10.1 us (53%)
  starting transfers between devices  5.21 us (27%)
  waiting for transfers between devices  3.02 us (16%)
  between operations  0.68 us (4%)
    ppermute x2, starting transfers between devices, shift(): lax.ppermute(x, 'mode', [(i, (i + by) % group) for i in range(group)])  5.14 us
    pallas_call x1, Pallas kernels, early(): pl.pallas_call(early_kernel, in_specs=[VMEM] + [HBM] * 4, out_shape=(pltp...  4.92 us
    ppermute x1, waiting for transfers between devices, shards(): lax.ppermute(edge, ('space', 'mode'), pairs + [(j, i) for i, j in pairs])  2.75 us
    pallas_call x1, Pallas kernels, transport(): pl.pallas_call(transport_kernel, in_specs=[VMEM] * (9 + len(others)), out...  1.59 us
    pallas_call x1, Pallas kernels, others_collision(): pl.pallas_call(others_kernel, in_specs=[VMEM] * 3, out_shape=(pltpu.VMEM(...  1.44 us
    pallas_call x1, Pallas kernels, coarsen(): pl.pallas_call(coarsen_kernel, in_specs=[HBM], out_shape=(pltpu.VMEM(stat...  1.07 us
    pallas_call x1, Pallas kernels, place_terms(): pl.pallas_call(place_kernel, in_specs=[VMEM] * 3, out_shape=jax.ShapeDtyp...  0.95 us
  transfers between devices with their start and end apart: 3, of which 2 were waited for; matrix products, arithmetic and copies ran while one was open for 0% of the time, Pallas kernels for 43%

profile of v1, /device:TPU:0, one launch (start us, length us, event | category | flops | bytes accessed | tf_op | source)
XLA Modules:
  0.0 19.0 jit_solution(13504203654228720426)
XLA Ops:
  0.6 1.1 %coarsen.1 = (bf16[858,128]{1,0:T(8,128)(2,1)S(1)}, f32[858,128]{1,0:T(8,128)S(1)}) custom-call(f32[858,128]{1,0:T(8,128)} %state_hbm.1), custom_call_target="tpu_custom_call" | custom-call | tf_op jit(solution)/shard_map/coarsen/pallas_call | solution.py:56
  1.7 3.0 %collective-permute-start.1 = (bf16[858,128]{1,0:T(8,128)(2,1)S(1)}, bf16[858,128]{1,0:T(8,128)(2,1)S(1)}, u32[]{:S(2)}, u32[]{:S(2)}) collective-permute-start(bf16[858,128]{1,0:T(8,128)(2,1)S(1)} %get-tuple-element.26.coarse_ref), channel_id=1, source_target_pairs={{0,1},{1,0},{2,3},{3,2},{4,5},{5,4},{6,7},{7,6},{8,9},{9,8},{10,11... | collective-permute-start | bytes 658952 | tf_op jit(solution)/shard_map/ppermute | solution.py:321
  4.7 4.9 %early_work.1 = (bf16[8,858]{1,0:T(8,128)(2,1)S(1)}, bf16[2288,858]{1,0:T(8,128)(2,1)S(1)}, f32[8,128]{1,0:T(8,128)S(1)}, bf16[286,286]{1,0:T(8,128)(2,1)S(1)}, ...) custom-call(bf16[858,128]{1,0:T(8,128)(2,1)S(1)} %get-tuple-element., ...), custom_call_target="tpu_custom_call" | custom-call | tf_op jit(solution)/shard_map/early_work/pallas_call | solution.py:206
  9.7 0.1 collective-permute-start
  9.7 0.1 late_work.1
  9.9 0.3 %collective-permute-done.1.coarse_ref.left_ref.right_ref = bf16[858,128]{1,0:T(8,128)(2,1)S(1)} collective-permute-done((bf16[858,128]{1,0:T(8,128)(2,1)S(1)}, bf16[858,128]{1,0:T(8,128)(2,1)S(1)}, u32[]{:S(2)}, u32[]{:S(2)}) %collective-permute-start.1) | collective-permute-done | bytes 219680 | tf_op jit(solution)/shard_map/ppermute | solution.py:321
  10.2 1.4 %others_collision.1 = (f32[8,128]{1,0:T(8,128)S(1)}, bf16[8,128]{1,0:T(8,128)(2,1)S(1)}) custom-call(bf16[2288,858]{1,0:T(8,128)(2,1)S(1)} %get-tuple-element.41.tensor_ref, bf16[858,128]{1,0:T(8,128)(2,1)S(1)} %collective-permute-done.1.coarse_ref.left_ref.right_ref, s32[8,128]{1,0:T(8,128)S(1)} %get-tuple-element.42.class_ref), custom_call_target="tpu_custom_call" | custom-call | tf_op jit(solution)/shard_map/others_collision/pallas_call | solution.py:240
  11.6 2.1 %collective-permute-start.2 = (bf16[8,128]{1,0:T(8,128)(2,1)S(1)}, bf16[8,128]{1,0:T(8,128)(2,1)S(1)}, u32[]{:S(2)}, u32[]{:S(2)}) collective-permute-start(bf16[8,128]{1,0:T(8,128)(2,1)S(1)} %get-tuple-element.46), channel_id=1, source_target_pairs={{0,1},{1,0},{2,3},{3,2},{4,5},{5,4},{6,7},{7,6},{8,9},{9,8},{10,11... | collective-permute-start | bytes 6152 | tf_op jit(solution)/shard_map/ppermute | solution.py:321
  13.7 2.8 %collective-permute-done.ring_ref = bf16[8,858]{1,0:T(8,128)(2,1)S(1)} collective-permute-done((bf16[8,858]{1,0:T(8,128)(2,1)S(1)}, bf16[8,858]{1,0:T(8,128)(2,1)S(1)}, u32[]{:S(2)}, u32[]{:S(2)}) %collective-permute-start) | collective-permute-done | bytes 13760 | tf_op jit(solution)/shard_map/ppermute | solution.py:331
  16.5 1.6 %transport.1 = (f32[858,128]{1,0:T(8,128)S(1)}, f32[8,256]{1,0:T(8,128)}) custom-call(f32[858,128]{1,0:T(8,128)S(1)} %get-tuple-element.25.state_ref, bf16[286,286]{1,0:T(8,128)(2,1)S(1)} %get-tuple-element.35.high_ref, bf16[286,286]{1,0:T(8,128)(2,1)S(1)} %get-tuple-element.36.low_ref, f32[8,128]{1,0:T(8,128)S(1)} %get-tuple-element.37.speed_ref, ...), custom_call_target="tpu_custom_call" | custom-call | tf_op jit(solution)/shard_map/transport/pallas_call | solution.py:289
  18.1 0.0 collective-permute-done.2.terms_ref
  18.1 1.0 %place_terms.1 = f32[858,128]{1,0:T(8,128)} custom-call(f32[858,128]{1,0:T(8,128)S(1)} %get-tuple-element.44.base_ref, bf16[858,8]{1,0:T(8,128)(2,1)S(1)} %get-tuple-element.45.there_ref, bf16[8,128]{1,0:T(8,128)(2,1)S(1)} %collective-permute-done.2.terms_ref), custom_call_target="tpu_custom_call" | custom-call | tf_op jit(solution)/shard_map/place_terms/pallas_call | solution.py:305
Async XLA Ops:
  1.7 8.5 %collective-permute-start.1 = (bf16[858,128]{1,0:T(8,128)(2,1)S(1)}, bf16[858,128]{1,0:T(8,128)(2,1)S(1)}, u32[]{:S(2)}, u32[]{:S(2)}) collective-permute-start(bf16[858,128]{1,0:T(8,128)(2,1)S(1)} %get-tuple-element.26.coarse_ref), channel_id=1, source_target_pairs={{0,1},{1,0},{2,3},{3,2},{4,5},{5,4},{6,7},{7,6},{8,9},{9,8},{10,11... | collective-permute-start | bytes 658952 | tf_op jit(solution)/shard_map/ppermute | solution.py:321
  9.7 6.8 %collective-permute-start = (bf16[8,858]{1,0:T(8,128)(2,1)S(1)}, bf16[8,858]{1,0:T(8,128)(2,1)S(1)}, u32[]{:S(2)}, u32[]{:S(2)}) collective-permute-start(bf16[8,858]{1,0:T(8,128)(2,1)S(1)} %get-tuple-element.38), channel_id=1, source_target_pairs={{1,2},{3,4},{5,6},{7,8},{9,10},{11,12},{13,14},{15,16},{17,18},{19... | collective-permute-start | bytes 41192 | tf_op jit(solution)/shard_map/ppermute | solution.py:331
  11.6 6.5 %collective-permute-start.2 = (bf16[8,128]{1,0:T(8,128)(2,1)S(1)}, bf16[8,128]{1,0:T(8,128)(2,1)S(1)}, u32[]{:S(2)}, u32[]{:S(2)}) collective-permute-start(bf16[8,128]{1,0:T(8,128)(2,1)S(1)} %get-tuple-element.46), channel_id=1, source_target_pairs={{0,1},{1,0},{2,3},{3,2},{4,5},{5,4},{6,7},{7,6},{8,9},{9,8},{10,11... | collective-permute-start | bytes 6152 | tf_op jit(solution)/shard_map/ppermute | solution.py:321

commit v2 on v1

v2 whole, which is shorter than its diff:
```python
import jax
import jax.numpy as jnp
from jax import lax
from jax.experimental import pallas as pl
from jax.experimental.pallas import tpu as pltpu
from jax.sharding import PartitionSpec as P

CLASSES = 3

wave_bound = 5.2
courant = 0.09
collision_update = 0.1

BF16 = jnp.bfloat16
F32 = jnp.float32
VMEM = pl.BlockSpec(memory_space=pltpu.VMEM)
HBM = pl.BlockSpec(memory_space=pltpu.HBM)
PARAMS = pltpu.CompilerParams(vmem_limit_bytes=16 * 2**20)


def remain(x):
    return pltpu.with_memory_space_constraint(x, pltpu.HBM)


def dot(a, b):
    return jnp.dot(a, b, preferred_element_type=F32)


def dot_general(a, b, da, db):
    return lax.dot_general(a, b, (((da,), (db,)), ((), ())), preferred_element_type=F32)


def halves(x):
    high = x.astype(BF16)
    return high, (x - high.astype(F32)).astype(BF16)


def iota(shape, axis):
    return lax.broadcasted_iota(jnp.int32, shape, axis)


def coarsen_kernel(state_hbm, coarse_ref, state_ref, sems):
    rows = state_ref.shape[0]
    cut = rows // 2 // 16 * 16
    copies = []
    for j, (start, size) in enumerate(((0, cut), (cut, rows - cut))):
        part = pl.ds(start, size)
        copies.append((part, pltpu.make_async_copy(state_hbm.at[part], state_ref.at[part], sems.at[j])))
        copies[-1][1].start()
    for part, copy in copies:
        copy.wait()
        coarse_ref[part] = state_ref[part].astype(BF16)


def coarsen(state):
    return pl.pallas_call(
        coarsen_kernel,
        in_specs=[HBM],
        out_shape=(pltpu.VMEM(state.shape, BF16), pltpu.VMEM(state.shape, F32)),
        out_specs=(VMEM,) * 2,
        scratch_shapes=[pltpu.SemaphoreType.DMA((2,))],
        compiler_params=PARAMS,
        name="coarsen",
    )(remain(state))


def steps_of(modes, terms):
    for count in range(min(32, modes), 0, -1):
        if modes % count == 0 and count * terms % 16 == 0:
            return modes // count
    return 1


def contract(tensor_ref, cells_ref, wide_ref, class_ref, steps):
    terms, columns = class_ref.shape[0], cells_ref.shape[1]
    modes = tensor_ref.shape[0] // terms
    wide_ref[...] = cells_ref[...].astype(F32)
    count = modes // steps
    sums = [jnp.zeros((terms, columns), F32) for _ in range(CLASSES)]
    for j in range(steps):
        product = dot(tensor_ref[pl.ds(j * count * terms, count * terms)], cells_ref[...])
        product = product.reshape(count, terms, columns)
        for c in range(CLASSES):
            first = wide_ref[pl.ds(c * modes + j * count, count)]
            sums[c] = sums[c] + jnp.sum(first[:, None, :] * product, axis=0)
    total = jnp.zeros((terms, columns), F32)
    for c in range(CLASSES):
        total = total + jnp.where(class_ref[:, 0:1] == c, sums[c], 0.0)
    return total


def advection_halves(table_ref, high_ref, low_ref):
    modes = table_ref.shape[1]
    index = [table_ref[j : j + 1, :].astype(F32) for j in range(3)]
    row = iota((8, modes), 0)
    weighted = jnp.where(row == 0, 144.0 * index[0], jnp.where(row == 1, 12.0 * index[1], index[2]))
    weighted = jnp.where(row < 3, weighted, 0.0).astype(BF16)
    along = jnp.where(row == 0, index[0], 0.0).astype(BF16)
    ones = jnp.ones((8, modes), BF16)
    code_down = dot_general(weighted, ones, 0, 0)
    along_down = dot_general(along, ones, 0, 0)
    code_across = 144.0 * index[0] + 12.0 * index[1] + index[2]
    matrix = jnp.where(code_across == code_down - 144.0, jnp.sqrt(along_down), 0.0)
    matrix = matrix + jnp.where(code_across == code_down + 144.0, jnp.sqrt(along_down + 1.0), 0.0)
    high_ref[...], low_ref[...] = halves(matrix)


def fetch(hbm, outs, scratch):
    tensor_hbm, table_hbm, thermal_hbm, target_hbm = hbm
    tensor_ref, high_ref, low_ref, class_ref, here_ref, there_ref, speed_ref = outs
    table_ref, thermal_ref, target_ref, sems = scratch
    terms = class_ref.shape[0]
    modes = high_ref.shape[0]
    outputs = target_ref.shape[0]
    pairs = (table_hbm, table_ref), (target_hbm, target_ref), (thermal_hbm, thermal_ref)
    small = [pltpu.make_async_copy(source, target, sems.at[j]) for j, (source, target) in enumerate(pairs)]
    for copy in small:
        copy.start()
    whole = pltpu.make_async_copy(tensor_hbm, tensor_ref, sems.at[len(small)])
    whole.start()
    for copy in small:
        copy.wait()
    first = lax.axis_index("mode") * terms
    for place_ref, start in ((here_ref, first), (there_ref, first + terms)):
        lane = iota(place_ref.shape, 1)
        target = jnp.zeros(place_ref.shape, jnp.int32)
        for j in range(place_ref.shape[1]):
            target = jnp.where(lane == j, target_ref[lax.rem(start + j, outputs)], target)
        place_ref[...] = (iota(place_ref.shape, 0) == target).astype(BF16)
    line = iota(class_ref.shape, 0)
    kind = jnp.zeros(class_ref.shape, jnp.int32)
    for j in range(terms):
        target = target_ref[first + j]
        own_class = sum((target >= c * modes).astype(jnp.int32) for c in range(1, CLASSES))
        kind = jnp.where(line == j, own_class, kind)
    class_ref[...] = kind
    line = iota(speed_ref.shape, 0)
    speed = jnp.zeros(speed_ref.shape, F32)
    for c in range(CLASSES):
        speed = jnp.where(line == c, thermal_ref[c], speed)
    speed_ref[...] = speed
    advection_halves(table_ref, high_ref, low_ref)
    whole.wait()


def at_seam():
    return jnp.logical_and(lax.axis_index("space") == 0, lax.axis_index("mode") == 0)


def early_kernel(coarse_ref, *refs):
    hbm, edge_ref, outs, scratch = refs[:4], refs[4], refs[5:12], refs[12:]
    rows, columns = coarse_ref.shape
    wanted = jnp.where(lax.axis_index("mode") == 0, 0, columns - 1)
    pick = (iota((8, columns), 1) == wanted).astype(BF16)
    edge = dot_general(pick, coarse_ref[...], 1, 1)
    lines = []
    for start in range(0, rows, columns):
        line = edge[0:1, start : min(start + columns, rows)]
        if line.shape[1] < columns:
            line = jnp.concatenate([line, jnp.zeros((1, columns - line.shape[1]), F32)], axis=1)
        lines.append(line)
    lines += [jnp.zeros((1, columns), F32)] * (edge_ref.shape[0] - len(lines))
    edge_ref[...] = jnp.concatenate(lines, axis=0).astype(BF16)

    @pl.when(at_seam())
    def _():
        fetch(hbm, outs, scratch)


def late_kernel(state_ref, *refs):
    hbm, outs, moved_ref, scratch, diff_ref = refs[:4], refs[11:18], refs[18], refs[19:-1], refs[-1]

    @pl.when(jnp.logical_not(at_seam()))
    def _():
        fetch(hbm, outs, scratch)

    inner_transport(state_ref, outs[1], outs[2], outs[6], moved_ref, diff_ref)


def inner_transport(state_ref, high_ref, low_ref, speed_ref, out_ref, diff_ref):
    rows, columns = state_ref.shape
    modes = high_ref.shape[0]
    state = state_ref[...]
    lane = iota((rows, columns), 1)
    before = jnp.where(lane == 0, 0.0, pltpu.roll(state, 1, 1))
    after = jnp.where(lane == columns - 1, 0.0, pltpu.roll(state, columns - 1, 1))
    diff_ref[...] = after - before
    out_ref[...] = before + after - 2.0 * state
    for c in range(CLASSES):
        part = pl.ds(c * modes, modes)
        speed = speed_ref[c : c + 1, :]
        d_high, d_low = halves(diff_ref[part])
        moved = dot(high_ref[...], d_high) + dot(high_ref[...], d_low) + dot(low_ref[...], d_high)
        diffused = (0.5 * wave_bound * courant) * out_ref[part]
        out_ref[part] = state_ref[part] + speed * (diffused - (0.5 * courant) * moved)


def held_shapes(tensor, state, modes, outputs):
    rows, columns = state.shape
    terms = tensor.shape[0] // modes
    return (
        pltpu.VMEM(tensor.shape, BF16),
        pltpu.VMEM((modes, modes), BF16),
        pltpu.VMEM((modes, modes), BF16),
        pltpu.VMEM((terms, columns), jnp.int32),
        pltpu.VMEM((rows, terms), BF16),
        pltpu.VMEM((rows, outputs - terms), BF16),
        pltpu.VMEM((8, columns), F32),
    )


def fetch_scratch(table, thermal, target):
    return [
        pltpu.VMEM(table.shape, jnp.int32),
        pltpu.SMEM(thermal.shape, F32),
        pltpu.SMEM(target.shape, jnp.int32),
        pltpu.SemaphoreType.DMA((4,)),
    ]


def early(coarse, tensor, table, thermal, target):
    rows, columns = coarse.shape
    shapes = held_shapes(tensor, coarse, table.shape[1], target.shape[0])
    lines = -(-rows // columns // 8) * 8
    return pl.pallas_call(
        early_kernel,
        in_specs=[VMEM] + [HBM] * 4,
        out_shape=(pltpu.VMEM((lines, columns), BF16),) + shapes,
        out_specs=(VMEM,) * (1 + len(shapes)),
        scratch_shapes=fetch_scratch(table, thermal, target),
        compiler_params=PARAMS,
        name="early_fetch",
    )(coarse, tensor, table, thermal, target)


def late(state, tensor, table, thermal, target, held):
    shapes = held_shapes(tensor, state, table.shape[1], target.shape[0])
    return pl.pallas_call(
        late_kernel,
        in_specs=[VMEM] + [HBM] * 4 + [VMEM] * len(held),
        out_shape=shapes + (pltpu.VMEM(state.shape, F32),),
        out_specs=(VMEM,) * (1 + len(shapes)),
        scratch_shapes=fetch_scratch(table, thermal, target) + [pltpu.VMEM(state.shape, F32)],
        input_output_aliases={5 + j: j for j in range(len(held))},
        compiler_params=PARAMS,
        name="late_fetch",
    )(state, tensor, table, thermal, target, *held)


def collide_kernel(tensor_ref, class_ref, *refs):
    sets = (len(refs) - 2) // 3 + 1
    given, totals, sent, (cells_ref, wide_ref) = refs[:sets], refs[sets : 2 * sets], refs[2 * sets : -2], refs[-2:]
    terms, columns = class_ref.shape
    for j, ref in enumerate(given):
        cells_ref[:, j * columns : (j + 1) * columns] = ref[...]
    total = contract(tensor_ref, cells_ref, wide_ref, class_ref, steps_of(tensor_ref.shape[0] // terms, terms))
    for j, ref in enumerate(totals):
        ref[...] = total[:, j * columns : (j + 1) * columns]
    for j, ref in enumerate(sent, 1):
        ref[...] = total[:, j * columns : (j + 1) * columns].astype(BF16)


def collide(tensor, class_of, cells):
    sets = len(cells)
    rows, columns = cells[0].shape
    shapes = [pltpu.VMEM(class_of.shape, F32)] * sets + [pltpu.VMEM(class_of.shape, BF16)] * (sets - 1)
    found = pl.pallas_call(
        collide_kernel,
        in_specs=[VMEM] * (2 + sets),
        out_shape=tuple(shapes),
        out_specs=(VMEM,) * len(shapes),
        scratch_shapes=[pltpu.VMEM((rows, sets * columns), t) for t in (BF16, F32)],
        compiler_params=PARAMS,
        name="collide",
    )(tensor, class_of, *cells)
    return found[:sets], found[sets:]


def ends_kernel(inner_ref, high_ref, low_ref, speed_ref, ring_ref, left_ref, right_ref, here_ref, *refs):
    totals, out_ref, collision_hbm, beyond_ref, collision_ref, sem = refs[:-5], *refs[-5:]
    rows, columns = inner_ref.shape
    modes = high_ref.shape[0]
    me, group = lax.axis_index("mode"), lax.axis_size("mode")
    for r, terms_ref in enumerate(totals):
        start = pl.multiple_of(lax.rem(me + group - r, group) * columns, columns)
        collision_ref[:, pl.ds(start, columns)] = terms_ref[...]
    copy = pltpu.make_async_copy(collision_ref, collision_hbm, sem)
    copy.start()
    lane = iota((rows, columns), 1)
    ring = []
    for j, start in enumerate(range(0, rows, columns)):
        one = (iota((ring_ref.shape[0], columns), 0) == j).astype(BF16)
        ring.append(dot_general(ring_ref[...], one, 0, 0)[0 : min(columns, rows - start)])
    ring = jnp.concatenate(ring, axis=0)
    left = jnp.where(me == 0, ring, pltpu.roll(left_ref[...].astype(F32), 1, 1))
    right = jnp.where(me == group - 1, ring, pltpu.roll(right_ref[...].astype(F32), columns - 1, 1))
    beyond_ref[...] = jnp.where(lane == 0, left, jnp.where(lane == columns - 1, right, 0.0))
    own_high, own_low = halves(totals[0][...])
    here = here_ref[...]
    out_ref[...] = inner_ref[...] + collision_update * (dot(here, own_high) + dot(here, own_low))
    sign = jnp.where(iota((1, columns), 1) == 0, -1.0, 1.0)
    for c in range(CLASSES):
        part = pl.ds(c * modes, modes)
        speed = speed_ref[c : c + 1, :]
        value = beyond_ref[part]
        coarse = value.astype(BF16)
        moved = sign * (dot(high_ref[...], coarse) + dot(low_ref[...], coarse))
        out_ref[part] = out_ref[part] + speed * (
            (0.5 * wave_bound * courant) * value - (0.5 * courant) * moved
        )
    copy.wait()


def ends(inner, high, low, speed, ring, left, right, here, totals):
    terms, columns = totals[0].shape
    collision = (terms, len(totals) * columns)
    return pl.pallas_call(
        ends_kernel,
        in_specs=[VMEM] * (8 + len(totals)),
        out_shape=(pltpu.VMEM(inner.shape, F32), jax.ShapeDtypeStruct(collision, F32)),
        out_specs=(VMEM, HBM),
        scratch_shapes=[pltpu.VMEM(inner.shape, F32), pltpu.VMEM(collision, F32), pltpu.SemaphoreType.DMA],
        compiler_params=PARAMS,
        name="ends",
    )(inner, high, low, speed, ring, left, right, here, *totals)


def place_kernel(base_ref, there_ref, terms_ref, out_ref):
    out_ref[...] = base_ref[...] + collision_update * dot(there_ref[...], terms_ref[...])


def place_terms(base, there, terms):
    return pl.pallas_call(
        place_kernel,
        in_specs=[VMEM] * 3,
        out_shape=jax.ShapeDtypeStruct(base.shape, F32),
        out_specs=VMEM,
        compiler_params=PARAMS,
        name="place_terms",
    )(base, there, terms)


def shards(state, tensor, table, thermal, output_mode_row):
    rows, columns = state.shape
    terms, modes, _ = tensor.shape
    slabs, group = lax.axis_size("space"), lax.axis_size("mode")

    def shift(x, by):
        return lax.ppermute(x, "mode", [(i, (i + by) % group) for i in range(group)])

    coarse, wide = coarsen(state)
    cells = {r: shift(coarse, r) for r in range(1, group)}

    flat = jnp.transpose(tensor, (1, 0, 2)).reshape(modes * terms, rows)
    given = tuple(remain(x) for x in (flat, table.T, thermal, output_mode_row))
    edge, *held = early(coarse, *given)
    size = slabs * group
    pairs = [(s * group + group - 1, (s + 1) * group % size) for s in range(slabs)]
    ring = lax.ppermute(edge, ("space", "mode"), pairs + [(j, i) for i, j in pairs])
    held_tensor, high, low, class_of, here, there, speed, inner = late(wide, *given, held)

    totals, sent = collide(held_tensor, class_of, [coarse] + [cells[r] for r in range(1, group)])
    returned = [shift(x, group - r) for r, x in enumerate(sent, 1)]
    base, collision = ends(
        inner, high, low, speed, ring, cells[1], cells[group - 1], here, totals
    )
    arrived = returned[0] if group == 2 else jnp.concatenate(returned)
    return place_terms(base, there, arrived), collision


def solution(mesh):
    in_specs = (P(None, ("space", "mode")), P("mode", None, None), P(), P(), P())
    out_specs = (P(None, ("space", "mode")), P("mode", "space"))
    return jax.shard_map(shards, mesh=mesh, in_specs=in_specs, out_specs=out_specs, check_vma=False)
```

time: 19.2 us -> 16.7 us (0.87)
  waiting for transfers between devices: 3.02 us -> 0.99 us
  Pallas kernels: 10.1 us -> 8.45 us
  starting transfers between devices: 5.21 us -> 6.4 us
    ppermute x1, waiting for transfers between devices: 2.75 us -> 0.06 us  [shards(): lax.ppermute(edge, ('space', 'mode'), pairs + [(j, i) for i, j in pairs])]
    pallas_call x1, Pallas kernels: 4.92 us -> 2.4 us  [early(): pl.pallas_call(early_kernel, in_specs=[VMEM] + [HBM] * 4, out_shape=(pltp...]
    ppermute x1, starting transfers between devices: 0.07 us -> 1.52 us  [shards(): lax.ppermute(edge, ('space', 'mode'), pairs + [(j, i) for i, j in pairs])]
    pallas_call x1, Pallas kernels: 0.15 us -> 0.88 us  [late(): pl.pallas_call(late_kernel, in_specs=[VMEM] + [HBM] * 4 + [VMEM] * len(he...]
    ppermute x2, waiting for transfers between devices: 0.27 us -> 0.94 us  [shift(): lax.ppermute(x, 'mode', [(i, (i + by) % group) for i in range(group)])]
    ppermute x2, starting transfers between devices: 5.14 us -> 4.88 us  [shift(): lax.ppermute(x, 'mode', [(i, (i + by) % group) for i in range(group)])]
  transfers between devices with their start and end apart: 3 -> 3, of which waited for: 2 -> 3; matrix products, arithmetic and copies ran while one was open for 0% -> 0% of each run, Pallas kernels for 43% -> 39%
where the time goes in v2:
time: 16.7 us; the launch traced here: 16.5 us
  Pallas kernels  8.45 us (51%)
  starting transfers between devices  6.4 us (38%)
  waiting for transfers between devices  0.99 us (6%)
  between operations  0.67 us (4%)
    ppermute x2, starting transfers between devices, shift(): lax.ppermute(x, 'mode', [(i, (i + by) % group) for i in range(group)])  4.88 us
    pallas_call x1, Pallas kernels, early(): pl.pallas_call(early_kernel, in_specs=[VMEM] + [HBM] * 4, out_shape=(pltp...  2.4 us
    pallas_call x1, Pallas kernels, collide(): pl.pallas_call(collide_kernel, in_specs=[VMEM] * (2 + sets), out_shape=tu...  1.73 us
    ppermute x1, starting transfers between devices, shards(): lax.ppermute(edge, ('space', 'mode'), pairs + [(j, i) for i, j in pairs])  1.52 us
    pallas_call x1, Pallas kernels, ends(): pl.pallas_call(ends_kernel, in_specs=[VMEM] * (8 + len(totals)), out_shap...  1.41 us
    pallas_call x1, Pallas kernels, coarsen(): pl.pallas_call(coarsen_kernel, in_specs=[HBM], out_shape=(pltpu.VMEM(stat...  1.07 us
    pallas_call x1, Pallas kernels, place_terms(): pl.pallas_call(place_kernel, in_specs=[VMEM] * 3, out_shape=jax.ShapeDtyp...  0.95 us
    ppermute x2, waiting for transfers between devices, shift(): lax.ppermute(x, 'mode', [(i, (i + by) % group) for i in range(group)])  0.94 us
  transfers between devices with their start and end apart: 3, of which 3 were waited for; matrix products, arithmetic and copies ran while one was open for 0% of the time, Pallas kernels for 39%

profile of v2, /device:TPU:0, one launch (start us, length us, event | category | flops | bytes accessed | tf_op | source)
XLA Modules:
  0.0 16.5 jit_solution(6757720093089774805)
XLA Ops:
  0.6 1.1 %coarsen.1 = (bf16[858,128]{1,0:T(8,128)(2,1)S(1)}, f32[858,128]{1,0:T(8,128)S(1)}) custom-call(f32[858,128]{1,0:T(8,128)} %state_hbm.1), custom_call_target="tpu_custom_call" | custom-call | tf_op jit(solution)/shard_map/coarsen/pallas_call | solution.py:56
  1.7 3.0 %collective-permute-start.1 = (bf16[858,128]{1,0:T(8,128)(2,1)S(1)}, bf16[858,128]{1,0:T(8,128)(2,1)S(1)}, u32[]{:S(2)}, u32[]{:S(2)}) collective-permute-start(bf16[858,128]{1,0:T(8,128)(2,1)S(1)} %get-tuple-element.26.coarse_ref.refs_0_), channel_id=1, source_target_pairs={{0,1},{1,0},{2,3},{3,2},{4,5},{5,4},{6,7},{7,6},{8,9},{9,8},{10,11... | collective-permute-start | bytes 658952 | tf_op jit(solution)/shard_map/ppermute | solution.py:349
  4.7 2.4 %early_fetch.1 = (bf16[8,128]{1,0:T(8,128)(2,1)S(1)}, bf16[2288,858]{1,0:T(8,128)(2,1)S(1)}, bf16[286,286]{1,0:T(8,128)(2,1)S(1)}, bf16[286,286]{1,0:T(8,128)(2,...) custom-call(bf16[858,128]{1,0:T(8,128)(2,1)S(1)} %get-tuple-element., ...), custom_call_target="tpu_custom_call" | custom-call | tf_op jit(solution)/shard_map/early_fetch/pallas_call | solution.py:225
  7.1 1.5 %collective-permute-start = (bf16[8,128]{1,0:T(8,128)(2,1)S(1)}, bf16[8,128]{1,0:T(8,128)(2,1)S(1)}, u32[]{:S(2)}, u32[]{:S(2)}) collective-permute-start(bf16[8,128]{1,0:T(8,128)(2,1)S(1)} %get-tuple-element.38), channel_id=1, source_target_pairs={{1,2},{3,4},{5,6},{7,8},{9,10},{11,12},{13,14},{15,16},{17,18},{19... | collective-permute-start | bytes 6152 | tf_op jit(solution)/shard_map/ppermute | solution.py:359
  8.7 0.9 %late_fetch.1 = (bf16[2288,858]{1,0:T(8,128)(2,1)S(1)}, bf16[286,286]{1,0:T(8,128)(2,1)S(1)}, bf16[286,286]{1,0:T(8,128)(2,1)S(1)}, s32[8,128]{1,0:T(8,128)S(1)}...) custom-call(f32[858,128]{1,0:T(8,128)S(1)} %get-tuple-element.25.sta, ...), custom_call_target="tpu_custom_call", output_to_operand_aliasing={{0}: (5, {}), {1}: (6, {}), {2}: (7, {}), {3}: (8, {}), {4}... | custom-call | tf_op jit(solution)/shard_map/late_fetch/pallas_call | solution.py:238
  9.6 0.6 %collective-permute-done.1.refs_1_.left_ref.right_ref = bf16[858,128]{1,0:T(8,128)(2,1)S(1)} collective-permute-done((bf16[858,128]{1,0:T(8,128)(2,1)S(1)}, bf16[858,128]{1,0:T(8,128)(2,1)S(1)}, u32[]{:S(2)}, u32[]{:S(2)}) %collective-permute-start.1) | collective-permute-done | bytes 219680 | tf_op jit(solution)/shard_map/ppermute | solution.py:349
  10.2 1.7 %collide.1 = (f32[8,128]{1,0:T(8,128)S(1)}, f32[8,128]{1,0:T(8,128)S(1)}, bf16[8,128]{1,0:T(8,128)(2,1)S(1)}) custom-call(bf16[2288,858]{1,0:T(8,128)(2,1)S(1)} %get-tuple-element.40.tensor_ref, s32[8,128]{1,0:T(8,128)S(1)} %get-tuple-element.41.class_ref, bf16[858,128]{1,0:T(8,128)(2,1)S(1)} %get-tuple-element.26.coarse_ref.refs_0_, ...), custom_call_target="tpu_custom_call" | custom-call | tf_op jit(solution)/shard_map/collide/pallas_call | solution.py:267
  11.9 1.8 %collective-permute-start.2 = (bf16[8,128]{1,0:T(8,128)(2,1)S(1)}, bf16[8,128]{1,0:T(8,128)(2,1)S(1)}, u32[]{:S(2)}, u32[]{:S(2)}) collective-permute-start(bf16[8,128]{1,0:T(8,128)(2,1)S(1)} %get-tuple-element.46), channel_id=1, source_target_pairs={{0,1},{1,0},{2,3},{3,2},{4,5},{5,4},{6,7},{7,6},{8,9},{9,8},{10,11... | collective-permute-start | bytes 6152 | tf_op jit(solution)/shard_map/ppermute | solution.py:349
  13.8 0.1 collective-permute-done.ring_ref
  13.8 1.4 %ends.1 = (f32[858,128]{1,0:T(8,128)S(1)}, f32[8,256]{1,0:T(8,128)}) custom-call(f32[858,128]{1,0:T(8,128)S(1)} %get-tuple-element.34.inner_ref, bf16[286,286]{1,0:T(8,128)(2,1)S(1)} %get-tuple-element.35.high_ref, bf16[286,286]{1,0:T(8,128)(2,1)S(1)} %get-tuple-element.36.low_ref, f32[8,128]{1,0:T(8,128)S(1)} %get-tuple-element.37.speed_ref, ...), custom_call_target="tpu_custom_call" | custom-call | tf_op jit(solution)/shard_map/ends/pallas_call | solution.py:317
  15.2 0.3 %collective-permute-done.2.terms_ref = bf16[8,128]{1,0:T(8,128)(2,1)S(1)} collective-permute-done((bf16[8,128]{1,0:T(8,128)(2,1)S(1)}, bf16[8,128]{1,0:T(8,128)(2,1)S(1)}, u32[]{:S(2)}, u32[]{:S(2)}) %collective-permute-start.2) | collective-permute-done | bytes 2080 | tf_op jit(solution)/shard_map/ppermute | solution.py:349
  15.6 1.0 %place_terms.1 = f32[858,128]{1,0:T(8,128)} custom-call(f32[858,128]{1,0:T(8,128)S(1)} %get-tuple-element.44.base_ref, bf16[858,8]{1,0:T(8,128)(2,1)S(1)} %get-tuple-element.45.there_ref, bf16[8,128]{1,0:T(8,128)(2,1)S(1)} %collective-permute-done.2.terms_ref), custom_call_target="tpu_custom_call" | custom-call | tf_op jit(solution)/shard_map/place_terms/pallas_call | solution.py:333
Async XLA Ops:
  1.7 8.5 %collective-permute-start.1 = (bf16[858,128]{1,0:T(8,128)(2,1)S(1)}, bf16[858,128]{1,0:T(8,128)(2,1)S(1)}, u32[]{:S(2)}, u32[]{:S(2)}) collective-permute-start(bf16[858,128]{1,0:T(8,128)(2,1)S(1)} %get-tuple-element.26.coarse_ref.refs_0_), channel_id=1, source_target_pairs={{0,1},{1,0},{2,3},{3,2},{4,5},{5,4},{6,7},{7,6},{8,9},{9,8},{10,11... | collective-permute-start | bytes 658952 | tf_op jit(solution)/shard_map/ppermute | solution.py:349
  7.1 6.7 %collective-permute-start = (bf16[8,128]{1,0:T(8,128)(2,1)S(1)}, bf16[8,128]{1,0:T(8,128)(2,1)S(1)}, u32[]{:S(2)}, u32[]{:S(2)}) collective-permute-start(bf16[8,128]{1,0:T(8,128)(2,1)S(1)} %get-tuple-element.38), channel_id=1, source_target_pairs={{1,2},{3,4},{5,6},{7,8},{9,10},{11,12},{13,14},{15,16},{17,18},{19... | collective-permute-start | bytes 6152 | tf_op jit(solution)/shard_map/ppermute | solution.py:359
  11.9 3.7 %collective-permute-start.2 = (bf16[8,128]{1,0:T(8,128)(2,1)S(1)}, bf16[8,128]{1,0:T(8,128)(2,1)S(1)}, u32[]{:S(2)}, u32[]{:S(2)}) collective-permute-start(bf16[8,128]{1,0:T(8,128)(2,1)S(1)} %get-tuple-element.46), channel_id=1, source_target_pairs={{0,1},{1,0},{2,3},{3,2},{4,5},{5,4},{6,7},{7,6},{8,9},{9,8},{10,11... | collective-permute-start | bytes 6152 | tf_op jit(solution)/shard_map/ppermute | solution.py:349

commit v3 on v0

v3 whole, which is shorter than its diff:
```python
import functools

import jax
import jax.numpy as jnp
from jax import lax
from jax.experimental import pallas as pl
from jax.experimental.pallas import tpu as pltpu
from jax.sharding import PartitionSpec as P

CLASSES = 3

wave_bound = 5.2
courant = 0.09
collision_update = 0.1

BF16 = jnp.bfloat16
F32 = jnp.float32
I32 = jnp.int32
VMEM = pl.BlockSpec(memory_space=pltpu.VMEM)
SMEM = pl.BlockSpec(memory_space=pltpu.SMEM)
HBM = pl.BlockSpec(memory_space=pltpu.HBM)
PARAMS = pltpu.CompilerParams(vmem_limit_bytes=16 * 2**20)


def remain(x):
    return pltpu.with_memory_space_constraint(x, pltpu.HBM)


def dot(a, b):
    return jnp.dot(a, b, preferred_element_type=F32)


def dot_general(a, b, da, db):
    return lax.dot_general(a, b, (((da,), (db,)), ((), ())), preferred_element_type=F32)


def halves(x):
    high = x.astype(BF16)
    return high, (x - high.astype(F32)).astype(BF16)


def iota(shape, axis):
    return lax.broadcasted_iota(I32, shape, axis)


def layout(rows, columns):
    cut = 5 * rows // 8 // 128 * 128
    tail = -(-(rows - cut) // 16) * 16
    lines = -(-rows // columns // 8) * 8
    return cut, tail, lines


def coarsen_kernel(state_hbm, *refs):
    small_hbm, head_ref, tail_ref, state_ref, small, sems = refs[:3], refs[3], refs[4], refs[5], refs[6:9], refs[9]
    rows, cut = state_ref.shape[0], head_ref.shape[0]
    parts = pl.ds(0, cut), pl.ds(cut, rows - cut)
    copies = [
        pltpu.make_async_copy(state_hbm.at[part], state_ref.at[part], sems.at[j])
        for j, part in enumerate(parts)
    ]
    copies += [
        pltpu.make_async_copy(source, target, sems.at[len(parts) + j])
        for j, (source, target) in enumerate(zip(small_hbm, small))
    ]
    for copy in copies:
        copy.start()
    copies[0].wait()
    head_ref[...] = state_ref[parts[0]].astype(BF16)
    copies[1].wait()
    tail = state_ref[parts[1]]
    tail_ref[...] = jnp.concatenate([tail, jnp.zeros((tail_ref.shape[0] - tail.shape[0], tail.shape[1]), F32)]).astype(BF16)
    for copy in copies[len(parts) :]:
        copy.wait()


def coarsen(state, table, thermal, target):
    rows, columns = state.shape
    cut, tail, lines = layout(rows, columns)
    return pl.pallas_call(
        coarsen_kernel,
        in_specs=[HBM] * 4,
        out_shape=(
            pltpu.VMEM((cut, columns), BF16),
            pltpu.VMEM((tail + 2 * lines, columns), BF16),
            pltpu.VMEM(state.shape, F32),
            pltpu.VMEM(table.shape, I32),
            pltpu.SMEM(thermal.shape, F32),
            pltpu.SMEM(target.shape, I32),
        ),
        out_specs=(VMEM, VMEM, VMEM, VMEM, SMEM, SMEM),
        scratch_shapes=[pltpu.SemaphoreType.DMA((5,))],
        compiler_params=PARAMS,
        name="coarsen",
    )(*(remain(x) for x in (state, table, thermal, target)))


def edges_kernel(head_ref, given_ref, tail_ref, ring_ref):
    cut, columns = head_ref.shape
    lines = ring_ref.shape[0]
    tail = tail_ref.shape[0] - 2 * lines
    rest = given_ref[0:tail]
    tail_ref[0:tail] = rest
    line, lane = iota((8, columns), 0), iota((8, columns), 1)
    pick = jnp.logical_or(
        jnp.logical_and(line == 0, lane == 0), jnp.logical_and(line == 1, lane == columns - 1)
    ).astype(BF16)
    found = jnp.concatenate([dot_general(pick, part, 1, 1) for part in (head_ref[...], rest)], axis=1)
    width = lines * columns
    found = jnp.concatenate([found, jnp.zeros((8, width - found.shape[1]), F32)], axis=1)
    folded = [
        jnp.concatenate([found[end : end + 1, j * columns : (j + 1) * columns] for j in range(lines)])
        for end in range(2)
    ]
    tail_ref[tail:] = jnp.concatenate(folded).astype(BF16)
    ring_ref[...] = jnp.where(lax.axis_index("mode") == 0, folded[0], folded[1]).astype(BF16)


def edges(rows, head, tail):
    columns = head.shape[1]
    return pl.pallas_call(
        edges_kernel,
        in_specs=[VMEM] * 2,
        out_shape=(pltpu.VMEM(tail.shape, BF16), pltpu.VMEM((layout(rows, columns)[2], columns), BF16)),
        out_specs=(VMEM,) * 2,
        compiler_params=PARAMS,
        name="edges",
    )(head, tail)


def advection_halves(table_ref, high_ref, low_ref):
    modes = table_ref.shape[1]
    index = [table_ref[j : j + 1, :].astype(F32) for j in range(3)]
    row = iota((8, modes), 0)
    weighted = jnp.where(row == 0, 144.0 * index[0], jnp.where(row == 1, 12.0 * index[1], index[2]))
    weighted = jnp.where(row < 3, weighted, 0.0).astype(BF16)
    along = jnp.where(row == 0, index[0], 0.0).astype(BF16)
    ones = jnp.ones((8, modes), BF16)
    code_down = dot_general(weighted, ones, 0, 0)
    along_down = dot_general(along, ones, 0, 0)
    code_across = 144.0 * index[0] + 12.0 * index[1] + index[2]
    matrix = jnp.where(code_across == code_down - 144.0, jnp.sqrt(along_down), 0.0)
    matrix = matrix + jnp.where(code_across == code_down + 144.0, jnp.sqrt(along_down + 1.0), 0.0)
    high_ref[...], low_ref[...] = halves(matrix)


def inner_transport(state_ref, high_ref, low_ref, thermal_ref, out_ref, diff_ref):
    rows, columns = state_ref.shape
    modes = high_ref.shape[0]
    state = state_ref[...]
    lane = iota((rows, columns), 1)
    before = jnp.where(lane == 0, 0.0, pltpu.roll(state, 1, 1))
    after = jnp.where(lane == columns - 1, 0.0, pltpu.roll(state, columns - 1, 1))
    diff_ref[...] = after - before
    out_ref[...] = before + after - 2.0 * state
    for c in range(CLASSES):
        part = pl.ds(c * modes, modes)
        d_high, d_low = halves(diff_ref[part])
        moved = dot(high_ref[...], d_high) + dot(high_ref[...], d_low) + dot(low_ref[...], d_high)
        diffused = (0.5 * wave_bound * courant) * out_ref[part]
        out_ref[part] = state_ref[part] + thermal_ref[c] * (diffused - (0.5 * courant) * moved)


def prepare(state_ref, table_ref, thermal_ref, tensor_hbm, outs, diff_ref, sem):
    tensor_ref, high_ref, low_ref, inner_ref = outs
    copy = pltpu.make_async_copy(tensor_hbm, tensor_ref, sem)
    copy.start()
    advection_halves(table_ref, high_ref, low_ref)
    inner_transport(state_ref, high_ref, low_ref, thermal_ref, inner_ref, diff_ref)
    copy.wait()


def at_seam():
    return jnp.logical_and(lax.axis_index("space") == 0, lax.axis_index("mode") == 0)


def early_kernel(ring_ref, state_ref, table_ref, thermal_ref, tensor_hbm, sent_ref, *refs):
    sent_ref[...] = ring_ref[...]

    @pl.when(at_seam())
    def _():
        prepare(state_ref, table_ref, thermal_ref, tensor_hbm, refs[:4], *refs[4:])


def late_kernel(state_ref, table_ref, thermal_ref, tensor_hbm, *refs):
    @pl.when(jnp.logical_not(at_seam()))
    def _():
        prepare(state_ref, table_ref, thermal_ref, tensor_hbm, refs[4:8], *refs[8:])


def held_shapes(tensor, state, modes):
    return (
        pltpu.VMEM(tensor.shape, BF16),
        pltpu.VMEM((modes, modes), BF16),
        pltpu.VMEM((modes, modes), BF16),
        pltpu.VMEM(state.shape, F32),
    )


def early(ring, state, table, thermal, tensor):
    shapes = (pltpu.VMEM(ring.shape, BF16),) + held_shapes(tensor, state, table.shape[1])
    return pl.pallas_call(
        early_kernel,
        in_specs=[VMEM, VMEM, VMEM, SMEM, HBM],
        out_shape=shapes,
        out_specs=(VMEM,) * len(shapes),
        scratch_shapes=[pltpu.VMEM(state.shape, F32), pltpu.SemaphoreType.DMA],
        compiler_params=PARAMS,
        name="early_prepare",
    )(ring, state, table, thermal, tensor)


def late(state, table, thermal, tensor, held):
    shapes = held_shapes(tensor, state, table.shape[1])
    return pl.pallas_call(
        late_kernel,
        in_specs=[VMEM, VMEM, SMEM, HBM] + [VMEM] * len(held),
        out_shape=shapes,
        out_specs=(VMEM,) * len(shapes),
        scratch_shapes=[pltpu.VMEM(state.shape, F32), pltpu.SemaphoreType.DMA],
        input_output_aliases={4 + j: j for j in range(len(held))},
        compiler_params=PARAMS,
        name="late_prepare",
    )(state, table, thermal, tensor, *held)


def classes(target_ref, first, shape, modes):
    line = iota(shape, 0)
    kind = jnp.zeros(shape, I32)
    for j in range(shape[0]):
        target = target_ref[first + j]
        own_class = sum((target >= c * modes).astype(I32) for c in range(1, CLASSES))
        kind = jnp.where(line == j, own_class, kind)
    return kind


def first_missing(cut, modes, c):
    return min(modes, max(0, cut - c * modes))


def begin_kernel(sets, target_ref, tensor_ref, *refs):
    heads, outs = refs[:sets], refs[sets:]
    cut, columns = heads[0].shape
    for at in range(0, sets, 2):
        sums_ref, product_ref, first_ref, wide_ref = *outs[at // 2 * 3 : at // 2 * 3 + 3], refs[-1]
        pair = range(at, min(at + 2, sets))
        shape = sums_ref.shape
        terms = shape[0]
        modes = tensor_ref.shape[0] // terms
        kind = classes(target_ref, lax.axis_index("mode") * terms, shape, modes)
        for j in pair:
            wide_ref[:, (j - at) * columns : (j - at + 1) * columns] = heads[j][...].astype(F32)
        cells = jnp.concatenate([heads[j][...] for j in pair], axis=1)
        product = dot(tensor_ref[:, 0:cut], cells).reshape(modes, *shape)
        missing = [first_missing(cut, modes, c) for c in range(CLASSES)]
        sums = [jnp.zeros(shape, F32) for _ in range(2)]
        for i in range(modes):
            first = jnp.zeros(shape, F32)
            later = jnp.zeros(shape, F32)
            for c in range(CLASSES):
                if i < missing[c]:
                    row = jnp.broadcast_to(wide_ref[pl.ds(c * modes + i, 1), 0 : shape[1]], shape)
                    first = row if c == 0 else jnp.where(kind == c, row, first)
                else:
                    first = jnp.where(kind == c, 0.0, first)
                    later = jnp.where(kind == c, product[i], later)
            first_ref[pl.ds(i * terms, terms)] = first
            if i >= min(missing):
                product_ref[pl.ds((i - min(missing)) * terms, terms)] = later
            sums[i % 2] = sums[i % 2] + first * product[i]
        sums_ref[...] = sums[0] + sums[1]


def begin(target, tensor, modes, heads):
    cut, columns = heads[0].shape
    terms = tensor.shape[0] // modes
    missing = min(first_missing(cut, modes, c) for c in range(CLASSES))
    shapes = []
    for at in range(0, len(heads), 2):
        width = columns * len(heads[at : at + 2])
        lengths = terms, (modes - missing) * terms, modes * terms
        shapes += [pltpu.VMEM((length, width), F32) for length in lengths]
    return pl.pallas_call(
        functools.partial(begin_kernel, len(heads)),
        in_specs=[SMEM, VMEM] + [VMEM] * len(heads),
        out_shape=tuple(shapes),
        out_specs=(VMEM,) * len(shapes),
        scratch_shapes=[pltpu.VMEM((cut, 2 * columns), F32)],
        compiler_params=PARAMS,
        name="begin_collide",
    )(target, tensor, *heads)


def finish_kernel(sets, target_ref, tensor_ref, *refs):
    begun, refs = refs[: (sets + 1) // 2 * 3], refs[(sets + 1) // 2 * 3 :]
    tails, totals, sent, wide_ref = refs[:sets], refs[sets : 2 * sets], refs[2 * sets : -1], refs[-1]
    terms, columns = totals[0].shape
    modes = tensor_ref.shape[0] // terms
    rows, rest = tensor_ref.shape[1], wide_ref.shape[0]
    cut = rows - rest
    missing = [first_missing(cut, modes, c) for c in range(CLASSES)]
    for at in range(0, sets, 2):
        sums_ref, product_ref, first_ref = begun[at // 2 * 3 : at // 2 * 3 + 3]
        pair = range(at, min(at + 2, sets))
        shape = sums_ref.shape
        kind = classes(target_ref, lax.axis_index("mode") * terms, shape, modes)
        parts = [tails[j][0:rest] for j in pair]
        for j, part in enumerate(parts):
            wide_ref[:, j * columns : (j + 1) * columns] = part.astype(F32)
        product = dot(tensor_ref[:, cut:], jnp.concatenate(parts, axis=1)).reshape(modes, *shape)
        sums = [sums_ref[...], jnp.zeros(shape, F32)]
        for i in range(modes):
            first = first_ref[pl.ds(i * terms, terms)]
            whole = product[i]
            for c in range(CLASSES):
                if i >= missing[c]:
                    row = jnp.broadcast_to(wide_ref[pl.ds(c * modes + i - cut, 1), 0 : shape[1]], shape)
                    first = jnp.where(kind == c, row, first)
            if i >= min(missing):
                whole = whole + product_ref[pl.ds((i - min(missing)) * terms, terms)]
            sums[i % 2] = sums[i % 2] + first * whole
        total = sums[0] + sums[1]
        for j in pair:
            part = total[:, (j - at) * columns : (j - at + 1) * columns]
            totals[j][...] = part
            if j > 0:
                sent[j - 1][...] = part.astype(BF16)


def finish(target, tensor, modes, begun, tails):
    sets = len(tails)
    rows, columns = tensor.shape[1], tails[0].shape[1]
    terms = tensor.shape[0] // modes
    shapes = [pltpu.VMEM((terms, columns), F32)] * sets + [pltpu.VMEM((terms, columns), BF16)] * (sets - 1)
    found = pl.pallas_call(
        functools.partial(finish_kernel, sets),
        in_specs=[SMEM, VMEM] + [VMEM] * (len(begun) + sets),
        out_shape=tuple(shapes),
        out_specs=(VMEM,) * len(shapes),
        scratch_shapes=[pltpu.VMEM((rows - layout(rows, columns)[0], 2 * columns), F32)],
        compiler_params=PARAMS,
        name="finish_collide",
    )(target, tensor, *begun, *tails)
    return found[:sets], found[sets:]


def ends_kernel(target_ref, thermal_ref, inner_ref, high_ref, low_ref, ring_ref, left_ref, right_ref, *refs):
    totals, base_ref, collision_ref = refs[:-2], *refs[-2:]
    rows, columns = inner_ref.shape
    modes = high_ref.shape[0]
    lines = ring_ref.shape[0]
    me, group = lax.axis_index("mode"), lax.axis_size("mode")
    terms = totals[0].shape[0]
    for r, terms_ref in enumerate(totals):
        start = pl.multiple_of(lax.rem(me + group - r, group) * columns, columns)
        collision_ref[:, pl.ds(start, columns)] = terms_ref[...]
    for j in range(terms):
        row = pl.ds(target_ref[me * terms + j], 1)
        base_ref[row] = base_ref[row] + collision_update * totals[0][j : j + 1]
    tail = left_ref.shape[0] - 2 * lines
    ring = ring_ref[...].astype(F32)
    left = jnp.where(me == 0, ring, left_ref[tail + lines : tail + 2 * lines].astype(F32))
    right = jnp.where(me == group - 1, ring, right_ref[tail : tail + lines].astype(F32))
    ends_of = [
        jnp.concatenate([folded[j : j + 1] for j in range(-(-rows // columns))], axis=1) for folded in (left, right)
    ]
    line = iota((8, modes), 0)
    packed = jnp.zeros((8, modes), F32)
    for c in range(CLASSES):
        for side, end in enumerate(ends_of):
            packed = jnp.where(line == 2 * c + side, end[:, c * modes : (c + 1) * modes], packed)
    coarse = packed.astype(BF16)
    moved = dot_general(high_ref[...], coarse, 1, 1) + dot_general(low_ref[...], coarse, 1, 1)
    lane = iota((1, 8), 1)
    speed = jnp.zeros((1, 8), F32)
    for c in range(CLASSES):
        speed = jnp.where(lane // 2 == c, thermal_ref[c], speed)
    sign = jnp.where(lane % 2 == 0, 1.0, -1.0)
    added = (0.5 * wave_bound * courant) * speed * packed.T + (0.5 * courant) * (sign * speed) * moved
    lane = iota((modes, columns), 1)
    for c in range(CLASSES):
        part = pl.ds(c * modes, modes)
        first = jnp.broadcast_to(added[:, 2 * c : 2 * c + 1], (modes, columns))
        last = jnp.broadcast_to(added[:, 2 * c + 1 : 2 * c + 2], (modes, columns))
        base_ref[part] = base_ref[part] + jnp.where(lane == 0, first, jnp.where(lane == columns - 1, last, 0.0))


def ends(target, thermal, inner, high, low, ring, left, right, totals):
    terms, columns = totals[0].shape
    return pl.pallas_call(
        ends_kernel,
        in_specs=[SMEM, SMEM] + [VMEM] * (6 + len(totals)),
        out_shape=(
            pltpu.VMEM(inner.shape, F32),
            pltpu.VMEM((terms, len(totals) * columns), F32),
        ),
        out_specs=(VMEM, VMEM),
        input_output_aliases={2: 0},
        compiler_params=PARAMS,
        name="ends",
    )(target, thermal, inner, high, low, ring, left, right, *totals)


def place_kernel(target_ref, _, *refs):
    arrived, (collision_ref, base_ref, out_hbm, collision_hbm, sems) = refs[:-5], refs[-5:]
    terms = arrived[0].shape[0]
    me, group = lax.axis_index("mode"), lax.axis_size("mode")
    copies = [pltpu.make_async_copy(collision_ref, collision_hbm, sems.at[0])]
    copies[0].start()
    for r, terms_ref in enumerate(arrived, 1):
        first = lax.rem(me + r, group) * terms
        values = collision_update * terms_ref[...].astype(F32)
        for j in range(terms):
            row = pl.ds(target_ref[first + j], 1)
            base_ref[row] = base_ref[row] + values[j : j + 1]
    copies.append(pltpu.make_async_copy(base_ref, out_hbm, sems.at[1]))
    copies[1].start()
    for copy in copies:
        copy.wait()


def place(target, base, arrived, collision):
    return pl.pallas_call(
        place_kernel,
        in_specs=[SMEM, VMEM] + [VMEM] * (len(arrived) + 1),
        out_shape=(
            pltpu.VMEM(base.shape, F32),
            jax.ShapeDtypeStruct(base.shape, F32),
            jax.ShapeDtypeStruct(collision.shape, F32),
        ),
        out_specs=(VMEM, HBM, HBM),
        scratch_shapes=[pltpu.SemaphoreType.DMA((2,))],
        input_output_aliases={1: 0},
        compiler_params=PARAMS,
        name="place",
    )(target, base, *arrived, collision)


def shards(state, tensor, table, thermal, output_mode_row):
    rows = state.shape[0]
    terms, modes, _ = tensor.shape
    slabs, group = lax.axis_size("space"), lax.axis_size("mode")

    def shift(x, by):
        return lax.ppermute(x, "mode", [(i, (i + by) % group) for i in range(group)])

    head, tail, wide, index, speed, target = coarsen(state, table.T, thermal, output_mode_row)
    heads = [head] + [shift(head, r) for r in range(1, group)]
    tail, ring = edges(rows, head, tail)
    tails = [tail] + [shift(tail, r) for r in range(1, group)]

    flat = remain(jnp.transpose(tensor, (1, 0, 2)).reshape(modes * terms, rows))
    ring, *held = early(ring, wide, index, speed, flat)
    size = slabs * group
    pairs = [(s * group + group - 1, (s + 1) * group % size) for s in range(slabs)]
    ring = lax.ppermute(ring, ("space", "mode"), pairs + [(j, i) for i, j in pairs])
    held_tensor, high, low, inner = late(wide, index, speed, flat, held)

    begun = begin(target, held_tensor, modes, heads)
    totals, sent = finish(target, held_tensor, modes, begun, tails)
    arrived = [shift(x, group - r) for r, x in enumerate(sent, 1)]
    base, collision = ends(target, speed, inner, high, low, ring, tails[1], tails[group - 1], totals)
    return place(target, base, arrived, collision)[1:]


def solution(mesh):
    in_specs = (P(None, ("space", "mode")), P("mode", None, None), P(), P(), P())
    out_specs = (P(None, ("space", "mode")), P("mode", "space"))
    return jax.shard_map(shards, mesh=mesh, in_specs=in_specs, out_specs=out_specs, check_vma=False)
```

time: 40.2 us -> 16.4 us (0.41)
  blocking collectives: 14.1 us -> 0 us
  matrix products: 9.8 us -> 0 us
  Pallas kernels: 0 us -> 6.77 us
  local copies, waits for them, and re-layouts: 4.69 us -> 0 us
  other arithmetic: 2.91 us -> 0 us
  waiting for transfers between devices: 0.01 us -> 1.59 us
  starting transfers between devices: 7.65 us -> 7.13 us
    all_gather x1 -> x0, blocking collectives: 14.1 us -> none  [shards(): slab = lax.all_gather(state, 'mode', axis=1, tiled=True)]
    dot_general x4 -> x0, matrix products: 9.8 us -> none  [the longest x1 3.63 us: shards(): jnp.dot(flat, piece, preferred_element_type=jnp.float32)]
    pallas_call x0 -> x8, Pallas kernels: none -> 6.77 us  [the longest x1 2.19 us: early(): pl.pallas_call(early_kernel, in_specs=[VMEM, VMEM, VMEM, SMEM, HBM], out_...]
    all_to_all x1 -> x0, starting transfers between devices: 3.21 us -> none  [shards(): lax.all_to_all(collision.astype(jnp.bfloat16), 'mode', split_axis=1, conc...]
    ppermute x2 -> x4, starting transfers between devices: 4.44 us -> 7.13 us  [the longest x3 4.38 us: shift(): lax.ppermute(x, 'mode', [(i, (i + by) % group) for i in range(group)])]
    unnamed x14 -> x0, local copies, waits for them, and re-layouts: 2.13 us -> none
    concatenate x1 -> x0, other arithmetic: 1.84 us -> none  [extended_2(): x = jnp.concatenate([before, x, after], axis=dim)]
    ppermute x2 -> x4, waiting for transfers between devices: 0.01 us -> 1.59 us  [the longest x1 0.87 us: shards(): lax.ppermute(ring, ('space', 'mode'), pairs + [(j, i) for i, j in pairs])]
  transfers between devices with their start and end apart: 3 -> 4, of which waited for: 0 -> 2; matrix products, arithmetic and copies ran while one was open for 35% -> 0% of each run, Pallas kernels for 0% -> 30%
where the time goes in v3:
time: 16.4 us; the launch traced here: 16.2 us
  starting transfers between devices  7.13 us (43%)
  Pallas kernels  6.77 us (41%)
  waiting for transfers between devices  1.59 us (10%)
  between operations  0.69 us (4%)
    ppermute x3, starting transfers between devices, shift(): lax.ppermute(x, 'mode', [(i, (i + by) % group) for i in range(group)])  4.38 us
    ppermute x1, starting transfers between devices, shards(): lax.ppermute(ring, ('space', 'mode'), pairs + [(j, i) for i, j in pairs])  2.74 us
    pallas_call x1, Pallas kernels, early(): pl.pallas_call(early_kernel, in_specs=[VMEM, VMEM, VMEM, SMEM, HBM], out_...  2.19 us
    pallas_call x1, Pallas kernels, coarsen(): pl.pallas_call(coarsen_kernel, in_specs=[HBM] * 4, out_shape=(pltpu.VMEM(...  1.07 us
    pallas_call x1, Pallas kernels, finish(): pl.pallas_call(functools.partial(finish_kernel, sets), in_specs=[SMEM, VM...  0.89 us
    ppermute x1, waiting for transfers between devices, shards(): lax.ppermute(ring, ('space', 'mode'), pairs + [(j, i) for i, j in pairs])  0.87 us
    pallas_call x1, Pallas kernels, begin(): pl.pallas_call(functools.partial(begin_kernel, len(heads)), in_specs=[SME...  0.86 us
    pallas_call x1, Pallas kernels, place(): pl.pallas_call(place_kernel, in_specs=[SMEM, VMEM] + [VMEM] * (len(arrive...  0.8 us
  transfers between devices with their start and end apart: 4, of which 2 were waited for; matrix products, arithmetic and copies ran while one was open for 0% of the time, Pallas kernels for 30%

profile of v3, /device:TPU:0, one launch (start us, length us, event | category | flops | bytes accessed | tf_op | source)
XLA Modules:
  0.0 16.2 jit_solution(12699760812519941939)
XLA Ops:
  0.6 1.1 %coarsen.1 = (bf16[512,128]{1,0:T(8,128)(2,1)S(1)}, bf16[368,128]{1,0:T(8,128)(2,1)S(1)}, f32[858,128]{1,0:T(8,128)S(1)}, s32[3,286]{1,0:T(4,128)S(1)}, f32[3]{0:T(128)S(4)}, /*index=5*/s32[16]{0:T(128)S(4)}) custom-call(f32[858,128]{1,0:T(8,128)} %state_hbm.1, s32[3,286]{1,0:T(4,128)} %bitcast.6, f32[3]{0:T(128)} %refs_1_.1, s32[16]{0:T(128)} %refs_2_.1), custom_call_target="tpu_custom_call" | custom-call | tf_op jit(solution)/shard_map/coarsen/pallas_call | solution.py:79
  1.7 3.0 %collective-permute-start.2 = (bf16[512,128]{1,0:T(8,128)(2,1)S(1)}, bf16[512,128]{1,0:T(8,128)(2,1)S(1)}, u32[]{:S(2)}, u32[]{:S(2)}) collective-permute-start(bf16[512,128]{1,0:T(8,128)(2,1)S(1)} %get-tuple-element.33.head_ref.refs_0_), channel_id=1, source_target_pairs={{0,1},{1,0},{2,3},{3,2},{4,5},{5,4},{6,7},{7,6},{8,9},{9,8},{10,11... | collective-permute-start | bytes 393224 | tf_op jit(solution)/shard_map/ppermute | solution.py:444
  4.7 0.2 %edges.1 = (bf16[368,128]{1,0:T(8,128)(2,1)S(1)}, bf16[8,128]{1,0:T(8,128)(2,1)S(1)}) custom-call(bf16[512,128]{1,0:T(8,128)(2,1)S(1)} %get-tuple-element.33.head_ref.refs_0_, bf16[368,128]{1,0:T(8,128)(2,1)S(1)} %get-tuple-element.34.given_ref), custom_call_target="tpu_custom_call" | custom-call | tf_op jit(solution)/shard_map/edges/pallas_call | solution.py:120
  4.9 0.1 collective-permute-start.1
  5.0 2.2 %early_prepare.1 = (bf16[8,128]{1,0:T(8,128)(2,1)S(1)}, bf16[2288,858]{1,0:T(8,128)(2,1)S(1)}, bf16[286,286]{1,0:T(8,128)(2,1)S(1)}, bf16[286,286]{1,0:T(8,128)(2,1)S(1)}, f32[858,128]{1,0:T(8,128)S(1)}) custom-call(bf16[8,128]{1,0:T(8,128)(2,1)S(1)} %get-tuple-element.35.ring_ref, f32[858,128]{1,0:T(8,128)S(1)} %get-tuple-element.31.state_ref, ...), custom_call_target="tpu_custom_call" | custom-call | tf_op jit(solution)/shard_map/early_prepare/pallas_call | solution.py:201
  7.2 2.7 %collective-permute-start = (bf16[8,128]{1,0:T(8,128)(2,1)S(1)}, bf16[8,128]{1,0:T(8,128)(2,1)S(1)}, u32[]{:S(2)}, u32[]{:S(2)}) collective-permute-start(bf16[8,128]{1,0:T(8,128)(2,1)S(1)} %get-tuple-element.43), channel_id=1, source_target_pairs={{1,2},{3,4},{5,6},{7,8},{9,10},{11,12},{13,14},{15,16},{17,18},{19... | collective-permute-start | bytes 6152 | tf_op jit(solution)/shard_map/ppermute | solution.py:455
  9.9 0.0 collective-permute-done.2.refs_1_
  10.0 0.9 %begin_collide.1 = (f32[8,256]{1,0:T(8,128)S(1)}, f32[2288,256]{1,0:T(8,128)S(1)}, f32[2288,256]{1,0:T(8,128)S(1)}) custom-call(s32[16]{0:T(128)S(4)} %get-tuple-element.29.target_ref, bf16[2288,858]{1,0:T(8,128)(2,1)S(1)} %get-tuple-element.45.tensor_ref, bf16[512,128]{1,0:T(8,128)(2,1)S(1)} %get-tuple-element.33.head_ref.refs_0_, ...), custom_call_target="tpu_custom_call" | custom-call | tf_op jit(solution)/shard_map/begin_collide/pallas_call | solution.py:282
  10.8 0.0 collective-permute-done.1.refs_4_.left_ref.right_ref
  10.8 0.9 %finish_collide.1 = (f32[8,128]{1,0:T(8,128)S(1)}, f32[8,128]{1,0:T(8,128)S(1)}, bf16[8,128]{1,0:T(8,128)(2,1)S(1)}) custom-call(s32[16]{0:T(128)S(4)} %get-tuple-element.29.target_ref, bf16[2288,858]{1,0:T(8,128)(2,1)S(1)} %get-tuple-element.45.tensor_ref, f32[8,256]{1,0:T(8,128)S(1)} %get-tuple-element.46.refs_0_, ...), custom_call_target="tpu_custom_call" | custom-call | tf_op jit(solution)/shard_map/finish_collide/pallas_call | solution.py:334
  11.7 1.3 %collective-permute-start.3 = (bf16[8,128]{1,0:T(8,128)(2,1)S(1)}, bf16[8,128]{1,0:T(8,128)(2,1)S(1)}, u32[]{:S(2)}, u32[]{:S(2)}) collective-permute-start(bf16[8,128]{1,0:T(8,128)(2,1)S(1)} %get-tuple-element.52), channel_id=1, source_target_pairs={{0,1},{1,0},{2,3},{3,2},{4,5},{5,4},{6,7},{7,6},{8,9},{9,8},{10,11... | collective-permute-start | bytes 6152 | tf_op jit(solution)/shard_map/ppermute | solution.py:444
  13.0 0.9 %collective-permute-done.ring_ref = bf16[8,128]{1,0:T(8,128)(2,1)S(1)} collective-permute-done((bf16[8,128]{1,0:T(8,128)(2,1)S(1)}, bf16[8,128]{1,0:T(8,128)(2,1)S(1)}, u32[]{:S(2)}, u32[]{:S(2)}) %collective-permute-start) | collective-permute-done | bytes 2080 | tf_op jit(solution)/shard_map/ppermute | solution.py:455
  13.9 0.8 %ends.1 = (f32[858,128]{1,0:T(8,128)S(1)}, f32[8,256]{1,0:T(8,128)S(1)}) custom-call(s32[16]{0:T(128)S(4)} %get-tuple-element.29.target_ref, f32[3]{0:T(128)S(4)} %get-tuple-element.30.thermal_ref, f32[858,128]{1,0:T(8,128)S(1)} %get-tuple-element.40.inner_ref, bf16[286,286]{1,0:T(8,128)(2,1)S(1)} %get-tuple-element.41.high_ref, ...), custom_call_target="tpu_custom_call", output_to_operand_aliasing={{0}: (2, {})} | custom-call | tf_op jit(solution)/shard_map/ends/pallas_call | solution.py:389
  14.7 0.7 %collective-permute-done.3.refs_0_ = bf16[8,128]{1,0:T(8,128)(2,1)S(1)} collective-permute-done((bf16[8,128]{1,0:T(8,128)(2,1)S(1)}, bf16[8,128]{1,0:T(8,128)(2,1)S(1)}, u32[]{:S(2)}, u32[]{:S(2)}) %collective-permute-start.3) | collective-permute-done | bytes 2080 | tf_op jit(solution)/shard_map/ppermute | solution.py:444
  15.4 0.8 %place.1 = (f32[858,128]{1,0:T(8,128)S(1)}, f32[858,128]{1,0:T(8,128)}, f32[8,256]{1,0:T(8,128)}) custom-call(s32[16]{0:T(128)S(4)} %get-tuple-element.29.target_ref, f32[858,128]{1,0:T(8,128)S(1)} %get-tuple-element.51._, bf16[8,128]{1,0:T(8,128)(2,1)S(1)} %collective-permute-done.3.refs_0_, ...), custom_call_target="tpu_custom_call", output_to_operand_aliasing={{0}: (1, {})} | custom-call | tf_op jit(solution)/shard_map/place/pallas_call | solution.py:422
  (1 shorter events, 0.0 us)
Async XLA Ops:
  1.7 8.2 %collective-permute-start.2 = (bf16[512,128]{1,0:T(8,128)(2,1)S(1)}, bf16[512,128]{1,0:T(8,128)(2,1)S(1)}, u32[]{:S(2)}, u32[]{:S(2)}) collective-permute-start(bf16[512,128]{1,0:T(8,128)(2,1)S(1)} %get-tuple-element.33.head_ref.refs_0_), channel_id=1, source_target_pairs={{0,1},{1,0},{2,3},{3,2},{4,5},{5,4},{6,7},{7,6},{8,9},{9,8},{10,11... | collective-permute-start | bytes 393224 | tf_op jit(solution)/shard_map/ppermute | solution.py:444
  4.9 5.9 %collective-permute-start.1 = (bf16[368,128]{1,0:T(8,128)(2,1)S(1)}, bf16[368,128]{1,0:T(8,128)(2,1)S(1)}, u32[]{:S(2)}, u32[]{:S(2)}) collective-permute-start(bf16[368,128]{1,0:T(8,128)(2,1)S(1)} %get-tuple-element.44.refs_3_), channel_id=1, source_target_pairs={{0,1},{1,0},{2,3},{3,2},{4,5},{5,4},{6,7},{7,6},{8,9},{9,8},{10,11... | collective-permute-start | bytes 282632 | tf_op jit(solution)/shard_map/ppermute | solution.py:444
  7.2 6.7 %collective-permute-start = (bf16[8,128]{1,0:T(8,128)(2,1)S(1)}, bf16[8,128]{1,0:T(8,128)(2,1)S(1)}, u32[]{:S(2)}, u32[]{:S(2)}) collective-permute-start(bf16[8,128]{1,0:T(8,128)(2,1)S(1)} %get-tuple-element.43), channel_id=1, source_target_pairs={{1,2},{3,4},{5,6},{7,8},{9,10},{11,12},{13,14},{15,16},{17,18},{19... | collective-permute-start | bytes 6152 | tf_op jit(solution)/shard_map/ppermute | solution.py:455
  11.7 3.7 %collective-permute-start.3 = (bf16[8,128]{1,0:T(8,128)(2,1)S(1)}, bf16[8,128]{1,0:T(8,128)(2,1)S(1)}, u32[]{:S(2)}, u32[]{:S(2)}) collective-permute-start(bf16[8,128]{1,0:T(8,128)(2,1)S(1)} %get-tuple-element.52), channel_id=1, source_target_pairs={{0,1},{1,0},{2,3},{3,2},{4,5},{5,4},{6,7},{7,6},{8,9},{9,8},{10,11... | collective-permute-start | bytes 6152 | tf_op jit(solution)/shard_map/ppermute | solution.py:444

commit v4 on v3

v4 whole, which is shorter than its diff:
```python
import jax
import jax.numpy as jnp
from jax import lax
from jax.experimental import pallas as pl
from jax.experimental.pallas import tpu as pltpu
from jax.sharding import PartitionSpec as P

CLASSES = 3

wave_bound = 5.2
courant = 0.09
collision_update = 0.1

BF16 = jnp.bfloat16
F32 = jnp.float32
I32 = jnp.int32
VMEM = pl.BlockSpec(memory_space=pltpu.VMEM)
SMEM = pl.BlockSpec(memory_space=pltpu.SMEM)
HBM = pl.BlockSpec(memory_space=pltpu.HBM)
PARAMS = pltpu.CompilerParams(vmem_limit_bytes=16 * 2**20)


def remain(x):
    return pltpu.with_memory_space_constraint(x, pltpu.HBM)


def dot(a, b):
    return jnp.dot(a, b, preferred_element_type=F32)


def dot_general(a, b, da, db):
    return lax.dot_general(a, b, (((da,), (db,)), ((), ())), preferred_element_type=F32)


def halves(x):
    high = x.astype(BF16)
    return high, (x - high.astype(F32)).astype(BF16)


def iota(shape, axis):
    return lax.broadcasted_iota(I32, shape, axis)


def coarsen_kernel(state_hbm, *refs):
    small_hbm, coarse_ref, state_ref, small, sems = refs[:3], refs[3], refs[4], refs[5:8], refs[8]
    rows = state_ref.shape[0]
    cut = rows // 2 // 16 * 16
    parts = pl.ds(0, cut), pl.ds(cut, rows - cut)
    copies = [
        pltpu.make_async_copy(state_hbm.at[part], state_ref.at[part], sems.at[j])
        for j, part in enumerate(parts)
    ]
    copies += [
        pltpu.make_async_copy(source, target, sems.at[len(parts) + j])
        for j, (source, target) in enumerate(zip(small_hbm, small))
    ]
    for copy in copies:
        copy.start()
    for part, copy in zip(parts, copies):
        copy.wait()
        coarse_ref[part] = state_ref[part].astype(BF16)
    for copy in copies[len(parts) :]:
        copy.wait()


def coarsen(state, table, thermal, target):
    return pl.pallas_call(
        coarsen_kernel,
        in_specs=[HBM] * 4,
        out_shape=(
            pltpu.VMEM(state.shape, BF16),
            pltpu.VMEM(state.shape, F32),
            pltpu.VMEM(table.shape, I32),
            pltpu.SMEM(thermal.shape, F32),
            pltpu.SMEM(target.shape, I32),
        ),
        out_specs=(VMEM, VMEM, VMEM, SMEM, SMEM),
        scratch_shapes=[pltpu.SemaphoreType.DMA((5,))],
        compiler_params=PARAMS,
        name="coarsen",
    )(*(remain(x) for x in (state, table, thermal, target)))


def advection_halves(table_ref, high_ref, low_ref):
    modes = table_ref.shape[1]
    index = [table_ref[j : j + 1, :].astype(F32) for j in range(3)]
    row = iota((8, modes), 0)
    weighted = jnp.where(row == 0, 144.0 * index[0], jnp.where(row == 1, 12.0 * index[1], index[2]))
    weighted = jnp.where(row < 3, weighted, 0.0).astype(BF16)
    along = jnp.where(row == 0, index[0], 0.0).astype(BF16)
    ones = jnp.ones((8, modes), BF16)
    code_down = dot_general(weighted, ones, 0, 0)
    along_down = dot_general(along, ones, 0, 0)
    code_across = 144.0 * index[0] + 12.0 * index[1] + index[2]
    matrix = jnp.where(code_across == code_down - 144.0, jnp.sqrt(along_down), 0.0)
    matrix = matrix + jnp.where(code_across == code_down + 144.0, jnp.sqrt(along_down + 1.0), 0.0)
    high_ref[...], low_ref[...] = halves(matrix)


def inner_transport(state_ref, high_ref, low_ref, thermal_ref, out_ref, diff_ref):
    rows, columns = state_ref.shape
    modes = high_ref.shape[0]
    state = state_ref[...]
    lane = iota((rows, columns), 1)
    before = jnp.where(lane == 0, 0.0, pltpu.roll(state, 1, 1))
    after = jnp.where(lane == columns - 1, 0.0, pltpu.roll(state, columns - 1, 1))
    diff_ref[...] = after - before
    out_ref[...] = before + after - 2.0 * state
    for c in range(CLASSES):
        part = pl.ds(c * modes, modes)
        d_high, d_low = halves(diff_ref[part])
        moved = dot(high_ref[...], d_high) + dot(high_ref[...], d_low) + dot(low_ref[...], d_high)
        diffused = (0.5 * wave_bound * courant) * out_ref[part]
        out_ref[part] = state_ref[part] + thermal_ref[c] * (diffused - (0.5 * courant) * moved)


def prepare(state_ref, table_ref, thermal_ref, target_ref, tensor_hbm, outs, diff_ref, sem):
    tensor_ref, high_ref, low_ref, inner_ref, kind_ref, own_ref = outs
    copy = pltpu.make_async_copy(tensor_hbm, tensor_ref, sem)
    modes = high_ref.shape[0]
    kind_ref[...] = classes(target_ref, lax.axis_index("mode") * kind_ref.shape[0], kind_ref.shape, modes)
    own_ref[...] = state_ref[...].astype(BF16).astype(F32)
    copy.start()
    advection_halves(table_ref, high_ref, low_ref)
    inner_transport(state_ref, high_ref, low_ref, thermal_ref, inner_ref, diff_ref)
    copy.wait()


FIRST, EARLY, LATE = range(3)


def stage():
    slab = lax.axis_index("space")
    return jnp.where(slab == 1, FIRST, jnp.where(slab == 0, EARLY, LATE))


def first_kernel(state_ref, table_ref, thermal_ref, target_ref, tensor_hbm, coarse_ref, *refs):
    @pl.when(stage() == FIRST)
    def _():
        prepare(state_ref, table_ref, thermal_ref, target_ref, tensor_hbm, refs[1:7], *refs[7:])


def early_kernel(state_ref, table_ref, thermal_ref, target_ref, tensor_hbm, coarse_ref, *refs):
    rows, columns = coarse_ref.shape
    edge_ref, refs = refs[6], refs[7:]
    wanted = jnp.where(lax.axis_index("mode") == 0, 0, columns - 1)
    pick = (iota((8, columns), 1) == wanted).astype(BF16)
    edge = dot_general(pick, coarse_ref[...], 1, 1)
    lines = edge_ref.shape[0]
    edge = jnp.concatenate([edge, jnp.zeros((8, lines * columns - rows), F32)], axis=1)
    folded = [edge[0:1, j * columns : (j + 1) * columns] for j in range(lines)]
    edge_ref[...] = jnp.concatenate(folded).astype(BF16)

    @pl.when(stage() == EARLY)
    def _():
        prepare(state_ref, table_ref, thermal_ref, target_ref, tensor_hbm, refs[:6], *refs[6:])


def late_kernel(state_ref, table_ref, thermal_ref, target_ref, tensor_hbm, *refs):
    @pl.when(stage() == LATE)
    def _():
        prepare(state_ref, table_ref, thermal_ref, target_ref, tensor_hbm, refs[6:12], *refs[12:])


def held_shapes(tensor, state, modes):
    return (
        pltpu.VMEM(tensor.shape, BF16),
        pltpu.VMEM((modes, modes), BF16),
        pltpu.VMEM((modes, modes), BF16),
        pltpu.VMEM(state.shape, F32),
        pltpu.VMEM((tensor.shape[0] // modes, 2 * state.shape[1]), I32),
        pltpu.VMEM(state.shape, F32),
    )


def preparing(kernel, state, table, thermal, target, tensor, coarse=None, held=None, extra=()):
    shapes = held_shapes(tensor, state, table.shape[1])
    given = [x for x in (coarse,) if x is not None] + list(held or ())
    inputs = 5 + (coarse is not None)
    aliases = {inputs + j: len(extra) + j for j in range(len(held or ()))}
    if kernel is first_kernel:
        aliases = {5: 0}
    return pl.pallas_call(
        kernel,
        in_specs=[VMEM, VMEM, SMEM, SMEM, HBM] + [VMEM] * len(given),
        out_shape=tuple(extra) + shapes,
        out_specs=(VMEM,) * (len(extra) + len(shapes)),
        scratch_shapes=[pltpu.VMEM(state.shape, F32), pltpu.SemaphoreType.DMA],
        input_output_aliases=aliases,
        compiler_params=PARAMS,
        name=kernel.__name__,
    )(state, table, thermal, target, tensor, *given)


def classes(target_ref, first, shape, modes):
    line = iota(shape, 0)
    kind = jnp.zeros(shape, I32)
    for j in range(shape[0]):
        target = target_ref[first + j]
        own_class = sum((target >= c * modes).astype(I32) for c in range(1, CLASSES))
        kind = jnp.where(line == j, own_class, kind)
    return kind


def contract(tensor_ref, cells, wide, kind):
    terms, columns = kind.shape
    modes = tensor_ref.shape[0] // terms
    product = dot(tensor_ref[...], cells).reshape(modes, terms, columns)
    sums = [jnp.zeros((terms, columns), F32) for _ in range(2)]

    def row(j):
        rows = [jnp.broadcast_to(ref[pl.ds(j, 1)], (terms, ref.shape[1])) for ref in wide]
        return jnp.concatenate(rows, axis=1)

    for i in range(modes):
        first = row(i)
        for c in range(1, CLASSES):
            first = jnp.where(kind == c, row(c * modes + i), first)
        sums[i % 2] = sums[i % 2] + first * product[i]
    return sums[0] + sums[1]


def collide_kernel(tensor_ref, kind_ref, own_ref, *refs):
    sets = len(refs) // 3
    given, totals, sent, wide_refs = refs[:sets], refs[sets : 2 * sets], refs[2 * sets : -1], refs[-1]
    columns = totals[0].shape[1]
    for at in range(0, sets, 2):
        pair = given[at : at + 2]
        cells = jnp.concatenate([ref[...] for ref in pair], axis=1)
        wide = []
        for j, ref in enumerate(pair):
            if at + j == 0:
                wide.append(own_ref)
            else:
                wide.append(wide_refs.at[j])
                wide_refs[j] = ref[...].astype(F32)
        total = contract(tensor_ref, cells, wide, kind_ref[:, 0 : len(pair) * columns])
        for j in range(len(pair)):
            part = total[:, j * columns : (j + 1) * columns]
            totals[at + j][...] = part
            if at + j > 0:
                sent[at + j - 1][...] = part.astype(BF16)


def collide(tensor, kind, own, cells):
    sets = len(cells)
    columns = cells[0].shape[1]
    terms = kind.shape[0]
    shapes = [pltpu.VMEM((terms, columns), F32)] * sets + [pltpu.VMEM((terms, columns), BF16)] * (sets - 1)
    found = pl.pallas_call(
        collide_kernel,
        in_specs=[VMEM] * (3 + sets),
        out_shape=tuple(shapes),
        out_specs=(VMEM,) * len(shapes),
        scratch_shapes=[pltpu.VMEM((2, *own.shape), F32)],
        compiler_params=PARAMS,
        name="collide",
    )(tensor, kind, own, *cells)
    return found[:sets], found[sets:]


def ends_kernel(target_ref, thermal_ref, inner_ref, high_ref, low_ref, ring_ref, left_ref, right_ref, *refs):
    totals, base_ref, collision_ref = refs[:-2], *refs[-2:]
    rows, columns = inner_ref.shape
    modes = high_ref.shape[0]
    me, group = lax.axis_index("mode"), lax.axis_size("mode")
    terms = totals[0].shape[0]
    for r, terms_ref in enumerate(totals):
        start = pl.multiple_of(lax.rem(me + group - r, group) * columns, columns)
        collision_ref[:, pl.ds(start, columns)] = terms_ref[...]
    for j in range(terms):
        row = pl.ds(target_ref[me * terms + j], 1)
        base_ref[row] = base_ref[row] + collision_update * totals[0][j : j + 1]
    line, lane = iota((8, columns), 0), iota((8, columns), 1)
    last = jnp.logical_and(line == 0, lane == columns - 1)
    first = jnp.logical_and(line == 1, lane == 0)
    if group == 2:
        beyond = dot_general(jnp.logical_or(last, first).astype(BF16), left_ref[...], 1, 1)
    else:
        beyond = dot_general(last.astype(BF16), left_ref[...], 1, 1)
        beyond = beyond + dot_general(first.astype(BF16), right_ref[...], 1, 1)
    ring = ring_ref[...].astype(F32)
    ring = jnp.concatenate([ring[j : j + 1] for j in range(-(-rows // columns))], axis=1)[:, 0:rows]
    ends_of = jnp.where(me == 0, ring, beyond[0:1]), jnp.where(me == group - 1, ring, beyond[1:2])
    line = iota((8, modes), 0)
    packed = jnp.zeros((8, modes), F32)
    for c in range(CLASSES):
        for side, end in enumerate(ends_of):
            packed = jnp.where(line == 2 * c + side, end[:, c * modes : (c + 1) * modes], packed)
    coarse = packed.astype(BF16)
    moved = dot_general(high_ref[...], coarse, 1, 1) + dot_general(low_ref[...], coarse, 1, 1)
    lane = iota((1, 8), 1)
    speed = jnp.zeros((1, 8), F32)
    for c in range(CLASSES):
        speed = jnp.where(lane // 2 == c, thermal_ref[c], speed)
    sign = jnp.where(lane % 2 == 0, 1.0, -1.0)
    added = (0.5 * wave_bound * courant) * speed * packed.T + (0.5 * courant) * (sign * speed) * moved
    lane = iota((modes, columns), 1)
    for c in range(CLASSES):
        part = pl.ds(c * modes, modes)
        first = jnp.broadcast_to(added[:, 2 * c : 2 * c + 1], (modes, columns))
        last = jnp.broadcast_to(added[:, 2 * c + 1 : 2 * c + 2], (modes, columns))
        base_ref[part] = base_ref[part] + jnp.where(lane == 0, first, jnp.where(lane == columns - 1, last, 0.0))


def ends(target, thermal, inner, high, low, ring, left, right, totals):
    terms, columns = totals[0].shape
    return pl.pallas_call(
        ends_kernel,
        in_specs=[SMEM, SMEM] + [VMEM] * (6 + len(totals)),
        out_shape=(
            pltpu.VMEM(inner.shape, F32),
            pltpu.VMEM((terms, len(totals) * columns), F32),
        ),
        out_specs=(VMEM, VMEM),
        input_output_aliases={2: 0},
        compiler_params=PARAMS,
        name="ends",
    )(target, thermal, inner, high, low, ring, left, right, *totals)


def place_kernel(target_ref, _, *refs):
    arrived, (collision_ref, base_ref, out_hbm, collision_hbm, sems) = refs[:-5], refs[-5:]
    terms = arrived[0].shape[0]
    me, group = lax.axis_index("mode"), lax.axis_size("mode")
    copies = [pltpu.make_async_copy(collision_ref, collision_hbm, sems.at[0])]
    for r, terms_ref in enumerate(arrived, 1):
        first = lax.rem(me + r, group) * terms
        values = collision_update * terms_ref[...].astype(F32)
        for j in range(terms):
            row = pl.ds(target_ref[first + j], 1)
            base_ref[row] = base_ref[row] + values[j : j + 1]
    copies.append(pltpu.make_async_copy(base_ref, out_hbm, sems.at[1]))
    copies[1].start()
    copies[0].start()
    for copy in copies:
        copy.wait()


def place(target, base, arrived, collision):
    return pl.pallas_call(
        place_kernel,
        in_specs=[SMEM, VMEM] + [VMEM] * (len(arrived) + 1),
        out_shape=(
            pltpu.VMEM(base.shape, F32),
            jax.ShapeDtypeStruct(base.shape, F32),
            jax.ShapeDtypeStruct(collision.shape, F32),
        ),
        out_specs=(VMEM, HBM, HBM),
        scratch_shapes=[pltpu.SemaphoreType.DMA((2,))],
        input_output_aliases={1: 0},
        compiler_params=PARAMS,
        name="place",
    )(target, base, *arrived, collision)


def shards(state, tensor, table, thermal, output_mode_row):
    rows = state.shape[0]
    terms, modes, _ = tensor.shape
    slabs, group = lax.axis_size("space"), lax.axis_size("mode")

    def shift(x, by):
        return lax.ppermute(x, "mode", [(i, (i + by) % group) for i in range(group)])

    columns = state.shape[1]
    flat = remain(jnp.transpose(tensor, (1, 0, 2)).reshape(modes * terms, rows))
    coarse, wide, index, speed, target = coarsen(state, table.T, thermal, output_mode_row)
    given = wide, index, speed, target, flat
    coarse, *held = preparing(first_kernel, *given, coarse, extra=[pltpu.VMEM(coarse.shape, BF16)])
    cells = [coarse] + [shift(coarse, r) for r in range(1, group)]

    lines = -(-rows // columns // 8) * 8
    edge, *held = preparing(early_kernel, *given, coarse, held, extra=[pltpu.VMEM((lines, columns), BF16)])
    size = slabs * group
    pairs = [(s * group + group - 1, (s + 1) * group % size) for s in range(slabs)]
    ring = lax.ppermute(edge, ("space", "mode"), pairs + [(j, i) for i, j in pairs])
    held_tensor, high, low, inner, kind, own = preparing(late_kernel, *given, held=held)

    totals, sent = collide(held_tensor, kind, own, cells)
    arrived = [shift(x, group - r) for r, x in enumerate(sent, 1)]
    base, collision = ends(target, speed, inner, high, low, ring, cells[1], cells[group - 1], totals)
    return place(target, base, arrived, collision)[1:]


def solution(mesh):
    in_specs = (P(None, ("space", "mode")), P("mode", None, None), P(), P(), P())
    out_specs = (P(None, ("space", "mode")), P("mode", "space"))
    return jax.shard_map(shards, mesh=mesh, in_specs=in_specs, out_specs=out_specs, check_vma=False)
```

time: 16.4 us -> 16.2 us (0.988)
    ppermute x1, starting transfers between devices: 2.74 us -> 1.52 us  [shards(): lax.ppermute(edge, ('space', 'mode'), pairs + [(j, i) for i, j in pairs])]
    ppermute x3 -> x2, starting transfers between devices: 4.38 us -> 5.46 us  [shift(): lax.ppermute(x, 'mode', [(i, (i + by) % group) for i in range(group)])]
    ppermute x3 -> x2, waiting for transfers between devices: 0.73 us -> 1.38 us  [shift(): lax.ppermute(x, 'mode', [(i, (i + by) % group) for i in range(group)])]
    ppermute x1, waiting for transfers between devices: 0.87 us -> 0.24 us  [shards(): lax.ppermute(edge, ('space', 'mode'), pairs + [(j, i) for i, j in pairs])]
    pallas_call x5 -> x4, Pallas kernels: 4.11 us -> 3.87 us  [the longest x3 2.41 us: preparing(): pl.pallas_call(kernel, in_specs=[VMEM, VMEM, SMEM, SMEM, HBM] + [VMEM] *...]
  transfers between devices with their start and end apart: 4 -> 3, of which waited for: 2 -> 3; matrix products, arithmetic and copies ran while one was open for 0% -> 0% of each run, Pallas kernels for 30% -> 30%
where the time goes in v4:
time: 16.2 us; the launch traced here: 16 us
  starting transfers between devices  6.98 us (43%)
  Pallas kernels  6.72 us (41%)
  waiting for transfers between devices  1.62 us (10%)
  between operations  0.68 us (4%)
    ppermute x2, starting transfers between devices, shift(): lax.ppermute(x, 'mode', [(i, (i + by) % group) for i in range(group)])  5.46 us
    pallas_call x3, Pallas kernels, preparing(): pl.pallas_call(kernel, in_specs=[VMEM, VMEM, SMEM, SMEM, HBM] + [VMEM] *...  2.41 us
    ppermute x1, starting transfers between devices, shards(): lax.ppermute(edge, ('space', 'mode'), pairs + [(j, i) for i, j in pairs])  1.52 us
    pallas_call x1, Pallas kernels, collide(): pl.pallas_call(collide_kernel, in_specs=[VMEM] * (3 + sets), out_shape=tu...  1.46 us
    ppermute x2, waiting for transfers between devices, shift(): lax.ppermute(x, 'mode', [(i, (i + by) % group) for i in range(group)])  1.38 us
    pallas_call x1, Pallas kernels, coarsen(): pl.pallas_call(coarsen_kernel, in_specs=[HBM] * 4, out_shape=(pltpu.VMEM(...  1.12 us
    pallas_call x1, Pallas kernels, ends(): pl.pallas_call(ends_kernel, in_specs=[SMEM, SMEM] + [VMEM] * (6 + len(tot...  0.94 us
    pallas_call x1, Pallas kernels, place(): pl.pallas_call(place_kernel, in_specs=[SMEM, VMEM] + [VMEM] * (len(arrive...  0.8 us
  transfers between devices with their start and end apart: 3, of which 3 were waited for; matrix products, arithmetic and copies ran while one was open for 0% of the time, Pallas kernels for 30%

profile of v4, /device:TPU:0, one launch (start us, length us, event | category | flops | bytes accessed | tf_op | source)
XLA Modules:
  0.0 16.0 jit_solution(11257150098218750125)
XLA Ops:
  0.6 1.1 %coarsen.1 = (bf16[858,128]{1,0:T(8,128)(2,1)S(1)}, f32[858,128]{1,0:T(8,128)S(1)}, s32[3,286]{1,0:T(4,128)S(1)}, f32[3]{0:T(128)S(4)}, s32[16]{0:T(128)S(4)}) custom-call(f32[858,128]{1,0:T(8,128)} %state_hbm.1, s32[3,286]{1,0:T(4,128)} %bitcast.7, f32[3]{0:T(128)} %refs_1_.1, s32[16]{0:T(128)} %refs_2_.1), custom_call_target="tpu_custom_call" | custom-call | tf_op jit(solution)/shard_map/coarsen/pallas_call | solution.py:67
  1.8 3.0 %collective-permute-start.1 = (bf16[858,128]{1,0:T(8,128)(2,1)S(1)}, bf16[858,128]{1,0:T(8,128)(2,1)S(1)}, u32[]{:S(2)}, u32[]{:S(2)}) collective-permute-start(bf16[858,128]{1,0:T(8,128)(2,1)S(1)} %get-tuple-element.39.coarse_ref.refs_0_), channel_id=1, source_target_pairs={{0,1},{1,0},{2,3},{3,2},{4,5},{5,4},{6,7},{7,6},{8,9},{9,8},{10,11... | collective-permute-start | bytes 658952 | tf_op jit(solution)/shard_map/ppermute | solution.py:363
  4.8 2.4 %early_kernel.1 = (bf16[8,128]{1,0:T(8,128)(2,1)S(1)}, bf16[2288,858]{1,0:T(8,128)(2,1)S(1)}, bf16[286,286]{1,0:T(8,128)(2,1)S(1)}, bf16[286,286]{1,0:T(8,128)(2...) custom-call(f32[858,128]{1,0:T(8,128)S(1)} %get-tuple-element.36.sta, ...), custom_call_target="tpu_custom_call", output_to_operand_aliasing={{1}: (6, {}), {2}: (7, {}), {3}: (8, {}), {4}: (9, {}), {5}... | custom-call | tf_op jit(solution)/shard_map/early_kernel/pallas_call | solution.py:183
  7.2 1.5 %collective-permute-start = (bf16[8,128]{1,0:T(8,128)(2,1)S(1)}, bf16[8,128]{1,0:T(8,128)(2,1)S(1)}, u32[]{:S(2)}, u32[]{:S(2)}) collective-permute-start(bf16[8,128]{1,0:T(8,128)(2,1)S(1)} %get-tuple-element.55), channel_id=1, source_target_pairs={{1,2},{3,4},{5,6},{7,8},{9,10},{11,12},{13,14},{15,16},{17,18},{19... | collective-permute-start | bytes 6152 | tf_op jit(solution)/shard_map/ppermute | solution.py:376
  8.7 1.0 %collective-permute-done.1.refs_1_.left_ref.right_ref = bf16[858,128]{1,0:T(8,128)(2,1)S(1)} collective-permute-done((bf16[858,128]{1,0:T(8,128)(2,1)S(1)}, bf16[858,128]{1,0:T(8,128)(2,1)S(1)}, u32[]{:S(2)}, u32[]{:S(2)}) %collective-permute-start.1) | collective-permute-done | bytes 219680 | tf_op jit(solution)/shard_map/ppermute | solution.py:363
  9.7 1.5 %collide.1 = (f32[8,128]{1,0:T(8,128)S(1)}, f32[8,128]{1,0:T(8,128)S(1)}, bf16[8,128]{1,0:T(8,128)(2,1)S(1)}) custom-call(bf16[2288,858]{1,0:T(8,128)(2,1)S(1)} %get-tuple-element.56.tensor_ref, s32[8,256]{1,0:T(8,128)S(1)} %get-tuple-element.57.kind_ref, f32[858,128]{1,0:T(8,128)S(1)} %get-tuple-element.58.own_ref, ...), custom_call_target="tpu_custom_call" | custom-call | tf_op jit(solution)/shard_map/collide/pallas_call | solution.py:250
  11.2 2.4 %collective-permute-start.2 = (bf16[8,128]{1,0:T(8,128)(2,1)S(1)}, bf16[8,128]{1,0:T(8,128)(2,1)S(1)}, u32[]{:S(2)}, u32[]{:S(2)}) collective-permute-start(bf16[8,128]{1,0:T(8,128)(2,1)S(1)} %get-tuple-element.62), channel_id=1, source_target_pairs={{0,1},{1,0},{2,3},{3,2},{4,5},{5,4},{6,7},{7,6},{8,9},{9,8},{10,11... | collective-permute-start | bytes 6152 | tf_op jit(solution)/shard_map/ppermute | solution.py:363
  13.6 0.2 %collective-permute-done.ring_ref = bf16[8,128]{1,0:T(8,128)(2,1)S(1)} collective-permute-done((bf16[8,128]{1,0:T(8,128)(2,1)S(1)}, bf16[8,128]{1,0:T(8,128)(2,1)S(1)}, u32[]{:S(2)}, u32[]{:S(2)}) %collective-permute-start) | collective-permute-done | bytes 2080 | tf_op jit(solution)/shard_map/ppermute | solution.py:376
  13.9 0.9 %ends.1 = (f32[858,128]{1,0:T(8,128)S(1)}, f32[8,256]{1,0:T(8,128)S(1)}) custom-call(s32[16]{0:T(128)S(4)} %get-tuple-element.34.target_ref, f32[3]{0:T(128)S(4)} %get-tuple-element.35.thermal_ref, f32[858,128]{1,0:T(8,128)S(1)} %get-tuple-element.52.inner_ref, bf16[286,286]{1,0:T(8,128)(2,1)S(1)} %get-tuple-element.53.high_ref, ...), custom_call_target="tpu_custom_call", output_to_operand_aliasing={{0}: (2, {})} | custom-call | tf_op jit(solution)/shard_map/ends/pallas_call | solution.py:308
  14.8 0.4 %collective-permute-done.2.refs_0_ = bf16[8,128]{1,0:T(8,128)(2,1)S(1)} collective-permute-done((bf16[8,128]{1,0:T(8,128)(2,1)S(1)}, bf16[8,128]{1,0:T(8,128)(2,1)S(1)}, u32[]{:S(2)}, u32[]{:S(2)}) %collective-permute-start.2) | collective-permute-done | bytes 2080 | tf_op jit(solution)/shard_map/ppermute | solution.py:363
  15.2 0.8 %place.1 = (f32[858,128]{1,0:T(8,128)S(1)}, f32[858,128]{1,0:T(8,128)}, f32[8,256]{1,0:T(8,128)}) custom-call(s32[16]{0:T(128)S(4)} %get-tuple-element.34.target_ref, f32[858,128]{1,0:T(8,128)S(1)} %get-tuple-element.61._, bf16[8,128]{1,0:T(8,128)(2,1)S(1)} %collective-permute-done.2.refs_0_, ...), custom_call_target="tpu_custom_call", output_to_operand_aliasing={{0}: (1, {})} | custom-call | tf_op jit(solution)/shard_map/place/pallas_call | solution.py:341
  (2 shorter events, 0.0 us)
Async XLA Ops:
  1.8 7.9 %collective-permute-start.1 = (bf16[858,128]{1,0:T(8,128)(2,1)S(1)}, bf16[858,128]{1,0:T(8,128)(2,1)S(1)}, u32[]{:S(2)}, u32[]{:S(2)}) collective-permute-start(bf16[858,128]{1,0:T(8,128)(2,1)S(1)} %get-tuple-element.39.coarse_ref.refs_0_), channel_id=1, source_target_pairs={{0,1},{1,0},{2,3},{3,2},{4,5},{5,4},{6,7},{7,6},{8,9},{9,8},{10,11... | collective-permute-start | bytes 658952 | tf_op jit(solution)/shard_map/ppermute | solution.py:363
  7.2 6.7 %collective-permute-start = (bf16[8,128]{1,0:T(8,128)(2,1)S(1)}, bf16[8,128]{1,0:T(8,128)(2,1)S(1)}, u32[]{:S(2)}, u32[]{:S(2)}) collective-permute-start(bf16[8,128]{1,0:T(8,128)(2,1)S(1)} %get-tuple-element.55), channel_id=1, source_target_pairs={{1,2},{3,4},{5,6},{7,8},{9,10},{11,12},{13,14},{15,16},{17,18},{19... | collective-permute-start | bytes 6152 | tf_op jit(solution)/shard_map/ppermute | solution.py:376
  11.2 4.0 %collective-permute-start.2 = (bf16[8,128]{1,0:T(8,128)(2,1)S(1)}, bf16[8,128]{1,0:T(8,128)(2,1)S(1)}, u32[]{:S(2)}, u32[]{:S(2)}) collective-permute-start(bf16[8,128]{1,0:T(8,128)(2,1)S(1)} %get-tuple-element.62), channel_id=1, source_target_pairs={{0,1},{1,0},{2,3},{3,2},{4,5},{5,4},{6,7},{7,6},{8,9},{9,8},{10,11... | collective-permute-start | bytes 6152 | tf_op jit(solution)/shard_map/ppermute | solution.py:363

commit v5 on v4

--- a/solution.py
+++ b/solution.py
@@ -42,7 +42,8 @@
 
 
 def coarsen_kernel(state_hbm, *refs):
-    small_hbm, coarse_ref, state_ref, small, sems = refs[:3], refs[3], refs[4], refs[5:8], refs[8]
+    small_hbm, tensor_hbm, coarse_ref, state_ref, small = refs[:3], refs[3], refs[4], refs[5], refs[6:9]
+    outs, (sems, *scratch) = refs[9:15], refs[15:]
     rows = state_ref.shape[0]
     cut = rows // 2 // 16 * 16
     parts = pl.ds(0, cut), pl.ds(cut, rows - cut)
@@ -62,23 +63,33 @@
     for copy in copies[len(parts) :]:
         copy.wait()
 
-
-def coarsen(state, table, thermal, target):
+    @pl.when(stage() == FIRST)
+    def _():
+        prepare(state_ref, *small, tensor_hbm, outs, *scratch)
+
+
+def coarsen(state, table, thermal, target, tensor):
+    shapes = (
+        pltpu.VMEM(state.shape, BF16),
+        pltpu.VMEM(state.shape, F32),
+        pltpu.VMEM(table.shape, I32),
+        pltpu.SMEM(thermal.shape, F32),
+        pltpu.SMEM(target.shape, I32),
+    )
+    held = held_shapes(tensor, state, table.shape[1])
     return pl.pallas_call(
         coarsen_kernel,
-        in_specs=[HBM] * 4,
-        out_shape=(
-            pltpu.VMEM(state.shape, BF16),
+        in_specs=[HBM] * 5,
+        out_shape=shapes + held,
+        out_specs=(VMEM, VMEM, VMEM, SMEM, SMEM) + (VMEM,) * len(held),
+        scratch_shapes=[
+            pltpu.SemaphoreType.DMA((5,)),
             pltpu.VMEM(state.shape, F32),
-            pltpu.VMEM(table.shape, I32),
-            pltpu.SMEM(thermal.shape, F32),
-            pltpu.SMEM(target.shape, I32),
-        ),
-        out_specs=(VMEM, VMEM, VMEM, SMEM, SMEM),
-        scratch_shapes=[pltpu.SemaphoreType.DMA((5,))],
+            pltpu.SemaphoreType.DMA,
+        ],
         compiler_params=PARAMS,
         name="coarsen",
-    )(*(remain(x) for x in (state, table, thermal, target)))
+    )(*(remain(x) for x in (state, table, thermal, target)), tensor)
 
 
 def advection_halves(table_ref, high_ref, low_ref):
@@ -134,12 +145,6 @@
     return jnp.where(slab == 1, FIRST, jnp.where(slab == 0, EARLY, LATE))
 
 
-def first_kernel(state_ref, table_ref, thermal_ref, target_ref, tensor_hbm, coarse_ref, *refs):
-    @pl.when(stage() == FIRST)
-    def _():
-        prepare(state_ref, table_ref, thermal_ref, target_ref, tensor_hbm, refs[1:7], *refs[7:])
-
-
 def early_kernel(state_ref, table_ref, thermal_ref, target_ref, tensor_hbm, coarse_ref, *refs):
     rows, columns = coarse_ref.shape
     edge_ref, refs = refs[6], refs[7:]
@@ -173,23 +178,19 @@
     )
 
 
-def preparing(kernel, state, table, thermal, target, tensor, coarse=None, held=None, extra=()):
-    shapes = held_shapes(tensor, state, table.shape[1])
-    given = [x for x in (coarse,) if x is not None] + list(held or ())
-    inputs = 5 + (coarse is not None)
-    aliases = {inputs + j: len(extra) + j for j in range(len(held or ()))}
-    if kernel is first_kernel:
-        aliases = {5: 0}
+def preparing(kernel, state, table, thermal, target, tensor, held, coarse=(), extra=()):
+    shapes = tuple(extra) + held_shapes(tensor, state, table.shape[1])
+    given = 5 + len(coarse)
     return pl.pallas_call(
         kernel,
-        in_specs=[VMEM, VMEM, SMEM, SMEM, HBM] + [VMEM] * len(given),
-        out_shape=tuple(extra) + shapes,
-        out_specs=(VMEM,) * (len(extra) + len(shapes)),
+        in_specs=[VMEM, VMEM, SMEM, SMEM, HBM] + [VMEM] * (len(coarse) + len(held)),
+        out_shape=shapes,
+        out_specs=(VMEM,) * len(shapes),
         scratch_shapes=[pltpu.VMEM(state.shape, F32), pltpu.SemaphoreType.DMA],
-        input_output_aliases=aliases,
+        input_output_aliases={given + j: len(extra) + j for j in range(len(held))},
         compiler_params=PARAMS,
         name=kernel.__name__,
-    )(state, table, thermal, target, tensor, *given)
+    )(state, table, thermal, target, tensor, *coarse, *held)
 
 
 def classes(target_ref, first, shape, modes):
@@ -364,17 +365,16 @@
 
     columns = state.shape[1]
     flat = remain(jnp.transpose(tensor, (1, 0, 2)).reshape(modes * terms, rows))
-    coarse, wide, index, speed, target = coarsen(state, table.T, thermal, output_mode_row)
+    coarse, wide, index, speed, target, *held = coarsen(state, table.T, thermal, output_mode_row, flat)
     given = wide, index, speed, target, flat
-    coarse, *held = preparing(first_kernel, *given, coarse, extra=[pltpu.VMEM(coarse.shape, BF16)])
     cells = [coarse] + [shift(coarse, r) for r in range(1, group)]
 
     lines = -(-rows // columns // 8) * 8
-    edge, *held = preparing(early_kernel, *given, coarse, held, extra=[pltpu.VMEM((lines, columns), BF16)])
+    edge, *held = preparing(early_kernel, *given, held, [coarse], extra=[pltpu.VMEM((lines, columns), BF16)])
     size = slabs * group
     pairs = [(s * group + group - 1, (s + 1) * group % size) for s in range(slabs)]
     ring = lax.ppermute(edge, ("space", "mode"), pairs + [(j, i) for i, j in pairs])
-    held_tensor, high, low, inner, kind, own = preparing(late_kernel, *given, held=held)
+    held_tensor, high, low, inner, kind, own = preparing(late_kernel, *given, held)
 
     totals, sent = collide(held_tensor, kind, own, cells)
     arrived = [shift(x, group - r) for r, x in enumerate(sent, 1)]

time: 16.2 us -> 16.1 us (level)
    pallas_call x3 -> x2, Pallas kernels: 2.41 us -> 2.38 us  [preparing(): pl.pallas_call(kernel, in_specs=[VMEM, VMEM, SMEM, SMEM, HBM] + [VMEM] *...]
where the time goes in v5:
time: 16.1 us; the launch traced here: 15.9 us
  starting transfers between devices  6.98 us (43%)
  Pallas kernels  6.65 us (41%)
  waiting for transfers between devices  1.62 us (10%)
  between operations  0.67 us (4%)
    ppermute x2, starting transfers between devices, shift(): lax.ppermute(x, 'mode', [(i, (i + by) % group) for i in range(group)])  5.46 us
    pallas_call x2, Pallas kernels, preparing(): pl.pallas_call(kernel, in_specs=[VMEM, VMEM, SMEM, SMEM, HBM] + [VMEM] *...  2.38 us
    ppermute x1, starting transfers between devices, shards(): lax.ppermute(edge, ('space', 'mode'), pairs + [(j, i) for i, j in pairs])  1.52 us
    pallas_call x1, Pallas kernels, collide(): pl.pallas_call(collide_kernel, in_specs=[VMEM] * (3 + sets), out_shape=tu...  1.39 us
    ppermute x2, waiting for transfers between devices, shift(): lax.ppermute(x, 'mode', [(i, (i + by) % group) for i in range(group)])  1.31 us
    pallas_call x1, Pallas kernels, coarsen(): pl.pallas_call(coarsen_kernel, in_specs=[HBM] * 5, out_shape=shapes + hel...  1.14 us
    pallas_call x1, Pallas kernels, ends(): pl.pallas_call(ends_kernel, in_specs=[SMEM, SMEM] + [VMEM] * (6 + len(tot...  0.94 us
    pallas_call x1, Pallas kernels, place(): pl.pallas_call(place_kernel, in_specs=[SMEM, VMEM] + [VMEM] * (len(arrive...  0.8 us
  transfers between devices with their start and end apart: 3, of which 3 were waited for; matrix products, arithmetic and copies ran while one was open for 0% of the time, Pallas kernels for 30%

profile of v5, /device:TPU:0, one launch (start us, length us, event | category | flops | bytes accessed | tf_op | source)
XLA Modules:
  0.0 15.9 jit_solution(1497839900011518031)
XLA Ops:
  0.6 1.1 %coarsen.1 = (bf16[858,128]{1,0:T(8,128)(2,1)S(1)}, f32[858,128]{1,0:T(8,128)S(1)}, s32[3,286]{1,0:T(4,128)S(1)}, f32[3]{0:T(128)S(4)}, s32[16]{0:T(128)S(4)}, /...) custom-call(f32[858,128]{1,0:T(8,128)} %state_hbm.1, ...), custom_call_target="tpu_custom_call" | custom-call | tf_op jit(solution)/shard_map/coarsen/pallas_call | solution.py:80
  1.8 3.0 %collective-permute-start.1 = (bf16[858,128]{1,0:T(8,128)(2,1)S(1)}, bf16[858,128]{1,0:T(8,128)(2,1)S(1)}, u32[]{:S(2)}, u32[]{:S(2)}) collective-permute-start(bf16[858,128]{1,0:T(8,128)(2,1)S(1)} %get-tuple-element.37.coarse_ref.refs_0_), channel_id=1, source_target_pairs={{0,1},{1,0},{2,3},{3,2},{4,5},{5,4},{6,7},{7,6},{8,9},{9,8},{10,11... | collective-permute-start | bytes 658952 | tf_op jit(solution)/shard_map/ppermute | solution.py:364
  4.8 2.4 %early_kernel.1 = (bf16[8,128]{1,0:T(8,128)(2,1)S(1)}, bf16[2288,858]{1,0:T(8,128)(2,1)S(1)}, bf16[286,286]{1,0:T(8,128)(2,1)S(1)}, bf16[286,286]{1,0:T(8,128)(2...) custom-call(f32[858,128]{1,0:T(8,128)S(1)} %get-tuple-element.35.sta, ...), custom_call_target="tpu_custom_call", output_to_operand_aliasing={{1}: (6, {}), {2}: (7, {}), {3}: (8, {}), {4}: (9, {}), {5}... | custom-call | tf_op jit(solution)/shard_map/early_kernel/pallas_call | solution.py:184
  7.2 1.5 %collective-permute-start = (bf16[8,128]{1,0:T(8,128)(2,1)S(1)}, bf16[8,128]{1,0:T(8,128)(2,1)S(1)}, u32[]{:S(2)}, u32[]{:S(2)}) collective-permute-start(bf16[8,128]{1,0:T(8,128)(2,1)S(1)} %get-tuple-element.53), channel_id=1, source_target_pairs={{1,2},{3,4},{5,6},{7,8},{9,10},{11,12},{13,14},{15,16},{17,18},{19... | collective-permute-start | bytes 6152 | tf_op jit(solution)/shard_map/ppermute | solution.py:376
  8.7 1.0 %collective-permute-done.1.refs_1_.left_ref.right_ref = bf16[858,128]{1,0:T(8,128)(2,1)S(1)} collective-permute-done((bf16[858,128]{1,0:T(8,128)(2,1)S(1)}, bf16[858,128]{1,0:T(8,128)(2,1)S(1)}, u32[]{:S(2)}, u32[]{:S(2)}) %collective-permute-start.1) | collective-permute-done | bytes 219680 | tf_op jit(solution)/shard_map/ppermute | solution.py:364
  9.7 1.4 %collide.1 = (f32[8,128]{1,0:T(8,128)S(1)}, f32[8,128]{1,0:T(8,128)S(1)}, bf16[8,128]{1,0:T(8,128)(2,1)S(1)}) custom-call(bf16[2288,858]{1,0:T(8,128)(2,1)S(1)} %get-tuple-element.54.tensor_ref, s32[8,256]{1,0:T(8,128)S(1)} %get-tuple-element.55.kind_ref, f32[858,128]{1,0:T(8,128)S(1)} %get-tuple-element.56.own_ref, ...), custom_call_target="tpu_custom_call" | custom-call | tf_op jit(solution)/shard_map/collide/pallas_call | solution.py:251
  11.1 2.4 %collective-permute-start.2 = (bf16[8,128]{1,0:T(8,128)(2,1)S(1)}, bf16[8,128]{1,0:T(8,128)(2,1)S(1)}, u32[]{:S(2)}, u32[]{:S(2)}) collective-permute-start(bf16[8,128]{1,0:T(8,128)(2,1)S(1)} %get-tuple-element.60), channel_id=1, source_target_pairs={{0,1},{1,0},{2,3},{3,2},{4,5},{5,4},{6,7},{7,6},{8,9},{9,8},{10,11... | collective-permute-start | bytes 6152 | tf_op jit(solution)/shard_map/ppermute | solution.py:364
  13.6 0.3 %collective-permute-done.ring_ref = bf16[8,128]{1,0:T(8,128)(2,1)S(1)} collective-permute-done((bf16[8,128]{1,0:T(8,128)(2,1)S(1)}, bf16[8,128]{1,0:T(8,128)(2,1)S(1)}, u32[]{:S(2)}, u32[]{:S(2)}) %collective-permute-start) | collective-permute-done | bytes 2080 | tf_op jit(solution)/shard_map/ppermute | solution.py:376
  13.9 0.9 %ends.1 = (f32[858,128]{1,0:T(8,128)S(1)}, f32[8,256]{1,0:T(8,128)S(1)}) custom-call(s32[16]{0:T(128)S(4)} %get-tuple-element.33.target_ref, f32[3]{0:T(128)S(4)} %get-tuple-element.34.thermal_ref, f32[858,128]{1,0:T(8,128)S(1)} %get-tuple-element.50.inner_ref, bf16[286,286]{1,0:T(8,128)(2,1)S(1)} %get-tuple-element.51.high_ref, ...), custom_call_target="tpu_custom_call", output_to_operand_aliasing={{0}: (2, {})} | custom-call | tf_op jit(solution)/shard_map/ends/pallas_call | solution.py:309
  14.8 0.3 %collective-permute-done.2.refs_0_ = bf16[8,128]{1,0:T(8,128)(2,1)S(1)} collective-permute-done((bf16[8,128]{1,0:T(8,128)(2,1)S(1)}, bf16[8,128]{1,0:T(8,128)(2,1)S(1)}, u32[]{:S(2)}, u32[]{:S(2)}) %collective-permute-start.2) | collective-permute-done | bytes 2080 | tf_op jit(solution)/shard_map/ppermute | solution.py:364
  15.1 0.8 %place.1 = (f32[858,128]{1,0:T(8,128)S(1)}, f32[858,128]{1,0:T(8,128)}, f32[8,256]{1,0:T(8,128)}) custom-call(s32[16]{0:T(128)S(4)} %get-tuple-element.33.target_ref, f32[858,128]{1,0:T(8,128)S(1)} %get-tuple-element.59._, bf16[8,128]{1,0:T(8,128)(2,1)S(1)} %collective-permute-done.2.refs_0_, ...), custom_call_target="tpu_custom_call", output_to_operand_aliasing={{0}: (1, {})} | custom-call | tf_op jit(solution)/shard_map/place/pallas_call | solution.py:342
  (1 shorter events, 0.0 us)
Async XLA Ops:
  1.8 7.9 %collective-permute-start.1 = (bf16[858,128]{1,0:T(8,128)(2,1)S(1)}, bf16[858,128]{1,0:T(8,128)(2,1)S(1)}, u32[]{:S(2)}, u32[]{:S(2)}) collective-permute-start(bf16[858,128]{1,0:T(8,128)(2,1)S(1)} %get-tuple-element.37.coarse_ref.refs_0_), channel_id=1, source_target_pairs={{0,1},{1,0},{2,3},{3,2},{4,5},{5,4},{6,7},{7,6},{8,9},{9,8},{10,11... | collective-permute-start | bytes 658952 | tf_op jit(solution)/shard_map/ppermute | solution.py:364
  7.2 6.7 %collective-permute-start = (bf16[8,128]{1,0:T(8,128)(2,1)S(1)}, bf16[8,128]{1,0:T(8,128)(2,1)S(1)}, u32[]{:S(2)}, u32[]{:S(2)}) collective-permute-start(bf16[8,128]{1,0:T(8,128)(2,1)S(1)} %get-tuple-element.53), channel_id=1, source_target_pairs={{1,2},{3,4},{5,6},{7,8},{9,10},{11,12},{13,14},{15,16},{17,18},{19... | collective-permute-start | bytes 6152 | tf_op jit(solution)/shard_map/ppermute | solution.py:376
  11.1 4.0 %collective-permute-start.2 = (bf16[8,128]{1,0:T(8,128)(2,1)S(1)}, bf16[8,128]{1,0:T(8,128)(2,1)S(1)}, u32[]{:S(2)}, u32[]{:S(2)}) collective-permute-start(bf16[8,128]{1,0:T(8,128)(2,1)S(1)} %get-tuple-element.60), channel_id=1, source_target_pairs={{0,1},{1,0},{2,3},{3,2},{4,5},{5,4},{6,7},{7,6},{8,9},{9,8},{10,11... | collective-permute-start | bytes 6152 | tf_op jit(solution)/shard_map/ppermute | solution.py:364

commit v6 on v5

--- a/solution.py
+++ b/solution.py
@@ -45,8 +45,7 @@
     small_hbm, tensor_hbm, coarse_ref, state_ref, small = refs[:3], refs[3], refs[4], refs[5], refs[6:9]
     outs, (sems, *scratch) = refs[9:15], refs[15:]
     rows = state_ref.shape[0]
-    cut = rows // 2 // 16 * 16
-    parts = pl.ds(0, cut), pl.ds(cut, rows - cut)
+    parts = [pl.ds(0, rows)]
     copies = [
         pltpu.make_async_copy(state_hbm.at[part], state_ref.at[part], sems.at[j])
         for j, part in enumerate(parts)
@@ -65,7 +64,7 @@
 
     @pl.when(stage() == FIRST)
     def _():
-        prepare(state_ref, *small, tensor_hbm, outs, *scratch)
+        prepare((state_ref, *small, tensor_hbm), outs, scratch, parts=2)
 
 
 def coarsen(state, table, thermal, target, tensor):
@@ -125,16 +124,24 @@
         out_ref[part] = state_ref[part] + thermal_ref[c] * (diffused - (0.5 * courant) * moved)
 
 
-def prepare(state_ref, table_ref, thermal_ref, target_ref, tensor_hbm, outs, diff_ref, sem):
+def prepare(given, outs, scratch, parts=1):
+    state_ref, table_ref, thermal_ref, target_ref, tensor_hbm = given
     tensor_ref, high_ref, low_ref, inner_ref, kind_ref, own_ref = outs
-    copy = pltpu.make_async_copy(tensor_hbm, tensor_ref, sem)
+    diff_ref, sem = scratch
     modes = high_ref.shape[0]
+    rows = tensor_ref.shape[0]
+    size = -(-rows // parts // 16) * 16
+    pieces = [pl.ds(start, min(size, rows - start)) for start in range(0, rows, size)]
+    copies = [pltpu.make_async_copy(tensor_hbm.at[piece], tensor_ref.at[piece], sem) for piece in pieces]
     kind_ref[...] = classes(target_ref, lax.axis_index("mode") * kind_ref.shape[0], kind_ref.shape, modes)
     own_ref[...] = state_ref[...].astype(BF16).astype(F32)
-    copy.start()
+    copies[0].start()
     advection_halves(table_ref, high_ref, low_ref)
     inner_transport(state_ref, high_ref, low_ref, thermal_ref, inner_ref, diff_ref)
-    copy.wait()
+    copies[0].wait()
+    for copy in copies[1:]:
+        copy.start()
+        copy.wait()
 
 
 FIRST, EARLY, LATE = range(3)
@@ -146,8 +153,17 @@
 
 
 def early_kernel(state_ref, table_ref, thermal_ref, target_ref, tensor_hbm, coarse_ref, *refs):
+    edge_ref, outs, scratch = refs[6], refs[7:13], refs[13:]
+    given = state_ref, table_ref, thermal_ref, target_ref, tensor_hbm
+    edge_row(coarse_ref, edge_ref)
+
+    @pl.when(stage() == EARLY)
+    def _():
+        prepare(given, outs, scratch)
+
+
+def edge_row(coarse_ref, edge_ref):
     rows, columns = coarse_ref.shape
-    edge_ref, refs = refs[6], refs[7:]
     wanted = jnp.where(lax.axis_index("mode") == 0, 0, columns - 1)
     pick = (iota((8, columns), 1) == wanted).astype(BF16)
     edge = dot_general(pick, coarse_ref[...], 1, 1)
@@ -156,15 +172,11 @@
     folded = [edge[0:1, j * columns : (j + 1) * columns] for j in range(lines)]
     edge_ref[...] = jnp.concatenate(folded).astype(BF16)
 
-    @pl.when(stage() == EARLY)
-    def _():
-        prepare(state_ref, table_ref, thermal_ref, target_ref, tensor_hbm, refs[:6], *refs[6:])
-
 
 def late_kernel(state_ref, table_ref, thermal_ref, target_ref, tensor_hbm, *refs):
     @pl.when(stage() == LATE)
     def _():
-        prepare(state_ref, table_ref, thermal_ref, target_ref, tensor_hbm, refs[6:12], *refs[12:])
+        prepare((state_ref, table_ref, thermal_ref, target_ref, tensor_hbm), refs[6:12], refs[12:])
 
 
 def held_shapes(tensor, state, modes):
@@ -260,10 +272,9 @@
     return found[:sets], found[sets:]
 
 
-def ends_kernel(target_ref, thermal_ref, inner_ref, high_ref, low_ref, ring_ref, left_ref, right_ref, *refs):
-    totals, base_ref, collision_ref = refs[:-2], *refs[-2:]
-    rows, columns = inner_ref.shape
-    modes = high_ref.shape[0]
+def own_ends_kernel(target_ref, inner_ref, left_ref, right_ref, *refs):
+    totals, base_ref, collision_ref, beyond_ref = refs[:-3], *refs[-3:]
+    columns = inner_ref.shape[1]
     me, group = lax.axis_index("mode"), lax.axis_size("mode")
     terms = totals[0].shape[0]
     for r, terms_ref in enumerate(totals):
@@ -280,6 +291,31 @@
     else:
         beyond = dot_general(last.astype(BF16), left_ref[...], 1, 1)
         beyond = beyond + dot_general(first.astype(BF16), right_ref[...], 1, 1)
+    beyond_ref[...] = beyond
+
+
+def own_ends(target, inner, left, right, totals):
+    terms, columns = totals[0].shape
+    return pl.pallas_call(
+        own_ends_kernel,
+        in_specs=[SMEM] + [VMEM] * (3 + len(totals)),
+        out_shape=(
+            pltpu.VMEM(inner.shape, F32),
+            pltpu.VMEM((terms, len(totals) * columns), F32),
+            pltpu.VMEM((8, inner.shape[0]), F32),
+        ),
+        out_specs=(VMEM,) * 3,
+        input_output_aliases={1: 0},
+        compiler_params=PARAMS,
+        name="own_ends",
+    )(target, inner, left, right, *totals)
+
+
+def ends_kernel(thermal_ref, inner_ref, high_ref, low_ref, ring_ref, beyond_ref, base_ref):
+    rows, columns = inner_ref.shape
+    modes = high_ref.shape[0]
+    me, group = lax.axis_index("mode"), lax.axis_size("mode")
+    beyond = beyond_ref[...]
     ring = ring_ref[...].astype(F32)
     ring = jnp.concatenate([ring[j : j + 1] for j in range(-(-rows // columns))], axis=1)[:, 0:rows]
     ends_of = jnp.where(me == 0, ring, beyond[0:1]), jnp.where(me == group - 1, ring, beyond[1:2])
@@ -304,20 +340,16 @@
         base_ref[part] = base_ref[part] + jnp.where(lane == 0, first, jnp.where(lane == columns - 1, last, 0.0))
 
 
-def ends(target, thermal, inner, high, low, ring, left, right, totals):
-    terms, columns = totals[0].shape
+def ends(thermal, inner, high, low, ring, beyond):
     return pl.pallas_call(
         ends_kernel,
-        in_specs=[SMEM, SMEM] + [VMEM] * (6 + len(totals)),
-        out_shape=(
-            pltpu.VMEM(inner.shape, F32),
-            pltpu.VMEM((terms, len(totals) * columns), F32),
-        ),
-        out_specs=(VMEM, VMEM),
-        input_output_aliases={2: 0},
+        in_specs=[SMEM] + [VMEM] * 5,
+        out_shape=pltpu.VMEM(inner.shape, F32),
+        out_specs=VMEM,
+        input_output_aliases={1: 0},
         compiler_params=PARAMS,
         name="ends",
-    )(target, thermal, inner, high, low, ring, left, right, *totals)
+    )(thermal, inner, high, low, ring, beyond)
 
 
 def place_kernel(target_ref, _, *refs):
@@ -378,7 +410,8 @@
 
     totals, sent = collide(held_tensor, kind, own, cells)
     arrived = [shift(x, group - r) for r, x in enumerate(sent, 1)]
-    base, collision = ends(target, speed, inner, high, low, ring, cells[1], cells[group - 1], totals)
+    base, collision, beyond = own_ends(target, inner, cells[1], cells[group - 1], totals)
+    base = ends(speed, base, high, low, ring, beyond)
     return place(target, base, arrived, collision)[1:]
 
 

time: 16.1 us -> 15.6 us (0.969)
  waiting for transfers between devices: 1.62 us -> 1.22 us
    ppermute x2, waiting for transfers between devices: 1.31 us -> 0.01 us  [shift(): lax.ppermute(x, 'mode', [(i, (i + by) % group) for i in range(group)])]
    ppermute x1, waiting for transfers between devices: 0.31 us -> 1.22 us  [shards(): lax.ppermute(edge, ('space', 'mode'), pairs + [(j, i) for i, j in pairs])]
    pallas_call x1 -> x2, Pallas kernels: 0.94 us -> 0.95 us  [the longest x1 0.79 us: ends(): pl.pallas_call(ends_kernel, in_specs=[SMEM] + [VMEM] * 5, out_shape=pltpu...]
  transfers between devices with their start and end apart: 3 -> 3, of which waited for: 3 -> 1; matrix products, arithmetic and copies ran while one was open for 0% -> 0% of each run, Pallas kernels for 30% -> 30%
where the time goes in v6:
time: 15.6 us; the launch traced here: 15.5 us
  starting transfers between devices  6.9 us (44%)
  Pallas kernels  6.67 us (43%)
  waiting for transfers between devices  1.22 us (8%)
  between operations  0.69 us (4%)
    ppermute x2, starting transfers between devices, shift(): lax.ppermute(x, 'mode', [(i, (i + by) % group) for i in range(group)])  5.37 us
    pallas_call x2, Pallas kernels, preparing(): pl.pallas_call(kernel, in_specs=[VMEM, VMEM, SMEM, SMEM, HBM] + [VMEM] *...  2.38 us
    ppermute x1, starting transfers between devices, shards(): lax.ppermute(edge, ('space', 'mode'), pairs + [(j, i) for i, j in pairs])  1.52 us
    pallas_call x1, Pallas kernels, collide(): pl.pallas_call(collide_kernel, in_specs=[VMEM] * (3 + sets), out_shape=tu...  1.39 us
    ppermute x1, waiting for transfers between devices, shards(): lax.ppermute(edge, ('space', 'mode'), pairs + [(j, i) for i, j in pairs])  1.22 us
    pallas_call x1, Pallas kernels, coarsen(): pl.pallas_call(coarsen_kernel, in_specs=[HBM] * 5, out_shape=shapes + hel...  1.13 us
    pallas_call x1, Pallas kernels, place(): pl.pallas_call(place_kernel, in_specs=[SMEM, VMEM] + [VMEM] * (len(arrive...  0.81 us
    pallas_call x1, Pallas kernels, ends(): pl.pallas_call(ends_kernel, in_specs=[SMEM] + [VMEM] * 5, out_shape=pltpu...  0.79 us
  transfers between devices with their start and end apart: 3, of which 1 were waited for; matrix products, arithmetic and copies ran while one was open for 0% of the time, Pallas kernels for 30%

profile of v6, /device:TPU:0, one launch (start us, length us, event | category | flops | bytes accessed | tf_op | source)
XLA Modules:
  0.0 15.5 jit_solution(16682821933020890845)
XLA Ops:
  0.6 1.1 %coarsen.1 = (bf16[858,128]{1,0:T(8,128)(2,1)S(1)}, f32[858,128]{1,0:T(8,128)S(1)}, s32[3,286]{1,0:T(4,128)S(1)}, f32[3]{0:T(128)S(4)}, s32[16]{0:T(128)S(4)}, /...) custom-call(f32[858,128]{1,0:T(8,128)} %state_hbm.1, ...), custom_call_target="tpu_custom_call" | custom-call | tf_op jit(solution)/shard_map/coarsen/pallas_call | solution.py:79
  1.8 3.0 %collective-permute-start = (bf16[858,128]{1,0:T(8,128)(2,1)S(1)}, bf16[858,128]{1,0:T(8,128)(2,1)S(1)}, u32[]{:S(2)}, u32[]{:S(2)}) collective-permute-start(bf16[858,128]{1,0:T(8,128)(2,1)S(1)} %get-tuple-element.38.coarse_ref.refs_0_), channel_id=1, source_target_pairs={{0,1},{1,0},{2,3},{3,2},{4,5},{5,4},{6,7},{7,6},{8,9},{9,8},{10,11... | collective-permute-start | bytes 658952 | tf_op jit(solution)/shard_map/ppermute | solution.py:396
  4.8 2.4 %early_kernel.1 = (bf16[8,128]{1,0:T(8,128)(2,1)S(1)}, bf16[2288,858]{1,0:T(8,128)(2,1)S(1)}, bf16[286,286]{1,0:T(8,128)(2,1)S(1)}, bf16[286,286]{1,0:T(8,128)(2...) custom-call(f32[858,128]{1,0:T(8,128)S(1)} %get-tuple-element.36.sta, ...), custom_call_target="tpu_custom_call", output_to_operand_aliasing={{1}: (6, {}), {2}: (7, {}), {3}: (8, {}), {4}: (9, {}), {5}... | custom-call | tf_op jit(solution)/shard_map/early_kernel/pallas_call | solution.py:196
  7.2 1.5 %collective-permute-start.1 = (bf16[8,128]{1,0:T(8,128)(2,1)S(1)}, bf16[8,128]{1,0:T(8,128)(2,1)S(1)}, u32[]{:S(2)}, u32[]{:S(2)}) collective-permute-start(bf16[8,128]{1,0:T(8,128)(2,1)S(1)} %get-tuple-element.60), channel_id=1, source_target_pairs={{1,2},{3,4},{5,6},{7,8},{9,10},{11,12},{13,14},{15,16},{17,18},{19... | collective-permute-start | bytes 6152 | tf_op jit(solution)/shard_map/ppermute | solution.py:408
  8.7 0.0 collective-permute-done.refs_1_.left_ref.right_ref
  8.7 1.4 %collide.1 = (f32[8,128]{1,0:T(8,128)S(1)}, f32[8,128]{1,0:T(8,128)S(1)}, bf16[8,128]{1,0:T(8,128)(2,1)S(1)}) custom-call(bf16[2288,858]{1,0:T(8,128)(2,1)S(1)} %get-tuple-element.52.tensor_ref, s32[8,256]{1,0:T(8,128)S(1)} %get-tuple-element.53.kind_ref, f32[858,128]{1,0:T(8,128)S(1)} %get-tuple-element.54.own_ref, ...), custom_call_target="tpu_custom_call" | custom-call | tf_op jit(solution)/shard_map/collide/pallas_call | solution.py:263
  10.1 2.3 %collective-permute-start.2 = (bf16[8,128]{1,0:T(8,128)(2,1)S(1)}, bf16[8,128]{1,0:T(8,128)(2,1)S(1)}, u32[]{:S(2)}, u32[]{:S(2)}) collective-permute-start(bf16[8,128]{1,0:T(8,128)(2,1)S(1)} %get-tuple-element.62), channel_id=1, source_target_pairs={{0,1},{1,0},{2,3},{3,2},{4,5},{5,4},{6,7},{7,6},{8,9},{9,8},{10,11... | collective-permute-start | bytes 6152 | tf_op jit(solution)/shard_map/ppermute | solution.py:396
  12.5 0.2 %own_ends.1 = (f32[858,128]{1,0:T(8,128)S(1)}, f32[8,256]{1,0:T(8,128)S(1)}, f32[8,858]{1,0:T(8,128)S(1)}) custom-call(s32[16]{0:T(128)S(4)} %get-tuple-element.34.target_ref, f32[858,128]{1,0:T(8,128)S(1)} %get-tuple-element.51.inner_ref, bf16[858,128]{1,0:T(8,128)(2,1)S(1)} %collective-permute-done.refs_1_.left_ref.right_ref, ...), custom_call_target="tpu_custom_call", output_to_operand_aliasing={{0}: (1, {})} | custom-call | tf_op jit(solution)/shard_map/own_ends/pallas_call | solution.py:299
  12.6 1.2 %collective-permute-done.1.ring_ref = bf16[8,128]{1,0:T(8,128)(2,1)S(1)} collective-permute-done((bf16[8,128]{1,0:T(8,128)(2,1)S(1)}, bf16[8,128]{1,0:T(8,128)(2,1)S(1)}, u32[]{:S(2)}, u32[]{:S(2)}) %collective-permute-start.1) | collective-permute-done | bytes 2080 | tf_op jit(solution)/shard_map/ppermute | solution.py:408
  13.8 0.8 %ends.1._ = f32[858,128]{1,0:T(8,128)S(1)} custom-call(f32[3]{0:T(128)S(4)} %get-tuple-element.35.thermal_ref, f32[858,128]{1,0:T(8,128)S(1)} %get-tuple-element.57.inner_ref, bf16[286,286]{1,0:T(8,128)(2,1)S(1)} %get-tuple-element.58.high_ref, bf16[286,286]{1,0:T(8,128)(2,1)S(1)} %get-tuple-element.59.low_ref, ...), custom_call_target="tpu_custom_call", output_to_operand_aliasing={{}: (1, {})} | custom-call | tf_op jit(solution)/shard_map/ends/pallas_call | solution.py:344
  14.6 0.0 collective-permute-done.2.refs_0_
  14.7 0.8 %place.1 = (f32[858,128]{1,0:T(8,128)S(1)}, f32[858,128]{1,0:T(8,128)}, f32[8,256]{1,0:T(8,128)}) custom-call(s32[16]{0:T(128)S(4)} %get-tuple-element.34.target_ref, f32[858,128]{1,0:T(8,128)S(1)} %ends.1._, bf16[8,128]{1,0:T(8,128)(2,1)S(1)} %collective-permute-done.2.refs_0_, f32[8,256]{1,0:T(8,128)S(1)} %get-tuple-element.63.refs_1_), custom_call_target="tpu_custom_call", output_to_operand_aliasing={{0}: (1, {})} | custom-call | tf_op jit(solution)/shard_map/place/pallas_call | solution.py:374
  (1 shorter events, 0.0 us)
Async XLA Ops:
  1.8 7.0 %collective-permute-start = (bf16[858,128]{1,0:T(8,128)(2,1)S(1)}, bf16[858,128]{1,0:T(8,128)(2,1)S(1)}, u32[]{:S(2)}, u32[]{:S(2)}) collective-permute-start(bf16[858,128]{1,0:T(8,128)(2,1)S(1)} %get-tuple-element.38.coarse_ref.refs_0_), channel_id=1, source_target_pairs={{0,1},{1,0},{2,3},{3,2},{4,5},{5,4},{6,7},{7,6},{8,9},{9,8},{10,11... | collective-permute-start | bytes 658952 | tf_op jit(solution)/shard_map/ppermute | solution.py:396
  7.2 6.7 %collective-permute-start.1 = (bf16[8,128]{1,0:T(8,128)(2,1)S(1)}, bf16[8,128]{1,0:T(8,128)(2,1)S(1)}, u32[]{:S(2)}, u32[]{:S(2)}) collective-permute-start(bf16[8,128]{1,0:T(8,128)(2,1)S(1)} %get-tuple-element.60), channel_id=1, source_target_pairs={{1,2},{3,4},{5,6},{7,8},{9,10},{11,12},{13,14},{15,16},{17,18},{19... | collective-permute-start | bytes 6152 | tf_op jit(solution)/shard_map/ppermute | solution.py:408
  10.1 4.5 %collective-permute-start.2 = (bf16[8,128]{1,0:T(8,128)(2,1)S(1)}, bf16[8,128]{1,0:T(8,128)(2,1)S(1)}, u32[]{:S(2)}, u32[]{:S(2)}) collective-permute-start(bf16[8,128]{1,0:T(8,128)(2,1)S(1)} %get-tuple-element.62), channel_id=1, source_target_pairs={{0,1},{1,0},{2,3},{3,2},{4,5},{5,4},{6,7},{7,6},{8,9},{9,8},{10,11... | collective-permute-start | bytes 6152 | tf_op jit(solution)/shard_map/ppermute | solution.py:396

commit v7 on v6

--- a/solution.py
+++ b/solution.py
@@ -332,12 +332,13 @@
         speed = jnp.where(lane // 2 == c, thermal_ref[c], speed)
     sign = jnp.where(lane % 2 == 0, 1.0, -1.0)
     added = (0.5 * wave_bound * courant) * speed * packed.T + (0.5 * courant) * (sign * speed) * moved
-    lane = iota((modes, columns), 1)
+    added = jnp.concatenate(halves(added), axis=1)
+    line, lane = iota((16, columns), 0) % 8, iota((16, columns), 1)
     for c in range(CLASSES):
         part = pl.ds(c * modes, modes)
-        first = jnp.broadcast_to(added[:, 2 * c : 2 * c + 1], (modes, columns))
-        last = jnp.broadcast_to(added[:, 2 * c + 1 : 2 * c + 2], (modes, columns))
-        base_ref[part] = base_ref[part] + jnp.where(lane == 0, first, jnp.where(lane == columns - 1, last, 0.0))
+        first = jnp.logical_and(line == 2 * c, lane == 0)
+        last = jnp.logical_and(line == 2 * c + 1, lane == columns - 1)
+        base_ref[part] = base_ref[part] + dot(added, jnp.logical_or(first, last).astype(BF16))
 
 
 def ends(thermal, inner, high, low, ring, beyond):

time: 15.6 us -> 15.6 us (level)
  no operation moved by 1% of the time
where the time goes in v7:
time: 15.6 us; the launch traced here: 15.4 us
  starting transfers between devices  6.9 us (44%)
  Pallas kernels  6.62 us (42%)
  waiting for transfers between devices  1.22 us (8%)
  between operations  0.69 us (4%)
    ppermute x2, starting transfers between devices, shift(): lax.ppermute(x, 'mode', [(i, (i + by) % group) for i in range(group)])  5.37 us
    pallas_call x2, Pallas kernels, preparing(): pl.pallas_call(kernel, in_specs=[VMEM, VMEM, SMEM, SMEM, HBM] + [VMEM] *...  2.38 us
    ppermute x1, starting transfers between devices, shards(): lax.ppermute(edge, ('space', 'mode'), pairs + [(j, i) for i, j in pairs])  1.52 us
    pallas_call x1, Pallas kernels, collide(): pl.pallas_call(collide_kernel, in_specs=[VMEM] * (3 + sets), out_shape=tu...  1.39 us
    ppermute x1, waiting for transfers between devices, shards(): lax.ppermute(edge, ('space', 'mode'), pairs + [(j, i) for i, j in pairs])  1.22 us
    pallas_call x1, Pallas kernels, coarsen(): pl.pallas_call(coarsen_kernel, in_specs=[HBM] * 5, out_shape=shapes + hel...  1.13 us
    pallas_call x1, Pallas kernels, place(): pl.pallas_call(place_kernel, in_specs=[SMEM, VMEM] + [VMEM] * (len(arrive...  0.81 us
    pallas_call x1, Pallas kernels, ends(): pl.pallas_call(ends_kernel, in_specs=[SMEM] + [VMEM] * 5, out_shape=pltpu...  0.75 us
  transfers between devices with their start and end apart: 3, of which 1 were waited for; matrix products, arithmetic and copies ran while one was open for 0% of the time, Pallas kernels for 30%

profile of v7, /device:TPU:0, one launch (start us, length us, event | category | flops | bytes accessed | tf_op | source)
XLA Modules:
  0.0 15.4 jit_solution(1131921953198136109)
XLA Ops:
  0.6 1.1 %coarsen.1 = (bf16[858,128]{1,0:T(8,128)(2,1)S(1)}, f32[858,128]{1,0:T(8,128)S(1)}, s32[3,286]{1,0:T(4,128)S(1)}, f32[3]{0:T(128)S(4)}, s32[16]{0:T(128)S(4)}, /...) custom-call(f32[858,128]{1,0:T(8,128)} %state_hbm.1, ...), custom_call_target="tpu_custom_call" | custom-call | tf_op jit(solution)/shard_map/coarsen/pallas_call | solution.py:79
  1.8 3.0 %collective-permute-start = (bf16[858,128]{1,0:T(8,128)(2,1)S(1)}, bf16[858,128]{1,0:T(8,128)(2,1)S(1)}, u32[]{:S(2)}, u32[]{:S(2)}) collective-permute-start(bf16[858,128]{1,0:T(8,128)(2,1)S(1)} %get-tuple-element.38.coarse_ref.refs_0_), channel_id=1, source_target_pairs={{0,1},{1,0},{2,3},{3,2},{4,5},{5,4},{6,7},{7,6},{8,9},{9,8},{10,11... | collective-permute-start | bytes 658952 | tf_op jit(solution)/shard_map/ppermute | solution.py:397
  4.8 2.4 %early_kernel.1 = (bf16[8,128]{1,0:T(8,128)(2,1)S(1)}, bf16[2288,858]{1,0:T(8,128)(2,1)S(1)}, bf16[286,286]{1,0:T(8,128)(2,1)S(1)}, bf16[286,286]{1,0:T(8,128)(2...) custom-call(f32[858,128]{1,0:T(8,128)S(1)} %get-tuple-element.36.sta, ...), custom_call_target="tpu_custom_call", output_to_operand_aliasing={{1}: (6, {}), {2}: (7, {}), {3}: (8, {}), {4}: (9, {}), {5}... | custom-call | tf_op jit(solution)/shard_map/early_kernel/pallas_call | solution.py:196
  7.2 1.5 %collective-permute-start.1 = (bf16[8,128]{1,0:T(8,128)(2,1)S(1)}, bf16[8,128]{1,0:T(8,128)(2,1)S(1)}, u32[]{:S(2)}, u32[]{:S(2)}) collective-permute-start(bf16[8,128]{1,0:T(8,128)(2,1)S(1)} %get-tuple-element.60), channel_id=1, source_target_pairs={{1,2},{3,4},{5,6},{7,8},{9,10},{11,12},{13,14},{15,16},{17,18},{19... | collective-permute-start | bytes 6152 | tf_op jit(solution)/shard_map/ppermute | solution.py:409
  8.7 0.0 collective-permute-done.refs_1_.left_ref.right_ref
  8.7 1.4 %collide.1 = (f32[8,128]{1,0:T(8,128)S(1)}, f32[8,128]{1,0:T(8,128)S(1)}, bf16[8,128]{1,0:T(8,128)(2,1)S(1)}) custom-call(bf16[2288,858]{1,0:T(8,128)(2,1)S(1)} %get-tuple-element.52.tensor_ref, s32[8,256]{1,0:T(8,128)S(1)} %get-tuple-element.53.kind_ref, f32[858,128]{1,0:T(8,128)S(1)} %get-tuple-element.54.own_ref, ...), custom_call_target="tpu_custom_call" | custom-call | tf_op jit(solution)/shard_map/collide/pallas_call | solution.py:263
  10.1 2.3 %collective-permute-start.2 = (bf16[8,128]{1,0:T(8,128)(2,1)S(1)}, bf16[8,128]{1,0:T(8,128)(2,1)S(1)}, u32[]{:S(2)}, u32[]{:S(2)}) collective-permute-start(bf16[8,128]{1,0:T(8,128)(2,1)S(1)} %get-tuple-element.62), channel_id=1, source_target_pairs={{0,1},{1,0},{2,3},{3,2},{4,5},{5,4},{6,7},{7,6},{8,9},{9,8},{10,11... | collective-permute-start | bytes 6152 | tf_op jit(solution)/shard_map/ppermute | solution.py:397
  12.5 0.2 %own_ends.1 = (f32[858,128]{1,0:T(8,128)S(1)}, f32[8,256]{1,0:T(8,128)S(1)}, f32[8,858]{1,0:T(8,128)S(1)}) custom-call(s32[16]{0:T(128)S(4)} %get-tuple-element.34.target_ref, f32[858,128]{1,0:T(8,128)S(1)} %get-tuple-element.51.inner_ref, bf16[858,128]{1,0:T(8,128)(2,1)S(1)} %collective-permute-done.refs_1_.left_ref.right_ref, ...), custom_call_target="tpu_custom_call", output_to_operand_aliasing={{0}: (1, {})} | custom-call | tf_op jit(solution)/shard_map/own_ends/pallas_call | solution.py:299
  12.6 1.2 %collective-permute-done.1.ring_ref = bf16[8,128]{1,0:T(8,128)(2,1)S(1)} collective-permute-done((bf16[8,128]{1,0:T(8,128)(2,1)S(1)}, bf16[8,128]{1,0:T(8,128)(2,1)S(1)}, u32[]{:S(2)}, u32[]{:S(2)}) %collective-permute-start.1) | collective-permute-done | bytes 2080 | tf_op jit(solution)/shard_map/ppermute | solution.py:409
  13.8 0.7 %ends.1._ = f32[858,128]{1,0:T(8,128)S(1)} custom-call(f32[3]{0:T(128)S(4)} %get-tuple-element.35.thermal_ref, f32[858,128]{1,0:T(8,128)S(1)} %get-tuple-element.57.inner_ref, bf16[286,286]{1,0:T(8,128)(2,1)S(1)} %get-tuple-element.58.high_ref, bf16[286,286]{1,0:T(8,128)(2,1)S(1)} %get-tuple-element.59.low_ref, ...), custom_call_target="tpu_custom_call", output_to_operand_aliasing={{}: (1, {})} | custom-call | tf_op jit(solution)/shard_map/ends/pallas_call | solution.py:345
  14.6 0.0 collective-permute-done.2.refs_0_
  14.6 0.8 %place.1 = (f32[858,128]{1,0:T(8,128)S(1)}, f32[858,128]{1,0:T(8,128)}, f32[8,256]{1,0:T(8,128)}) custom-call(s32[16]{0:T(128)S(4)} %get-tuple-element.34.target_ref, f32[858,128]{1,0:T(8,128)S(1)} %ends.1._, bf16[8,128]{1,0:T(8,128)(2,1)S(1)} %collective-permute-done.2.refs_0_, f32[8,256]{1,0:T(8,128)S(1)} %get-tuple-element.63.refs_1_), custom_call_target="tpu_custom_call", output_to_operand_aliasing={{0}: (1, {})} | custom-call | tf_op jit(solution)/shard_map/place/pallas_call | solution.py:375
  (1 shorter events, 0.0 us)
Async XLA Ops:
  1.8 7.0 %collective-permute-start = (bf16[858,128]{1,0:T(8,128)(2,1)S(1)}, bf16[858,128]{1,0:T(8,128)(2,1)S(1)}, u32[]{:S(2)}, u32[]{:S(2)}) collective-permute-start(bf16[858,128]{1,0:T(8,128)(2,1)S(1)} %get-tuple-element.38.coarse_ref.refs_0_), channel_id=1, source_target_pairs={{0,1},{1,0},{2,3},{3,2},{4,5},{5,4},{6,7},{7,6},{8,9},{9,8},{10,11... | collective-permute-start | bytes 658952 | tf_op jit(solution)/shard_map/ppermute | solution.py:397
  7.2 6.7 %collective-permute-start.1 = (bf16[8,128]{1,0:T(8,128)(2,1)S(1)}, bf16[8,128]{1,0:T(8,128)(2,1)S(1)}, u32[]{:S(2)}, u32[]{:S(2)}) collective-permute-start(bf16[8,128]{1,0:T(8,128)(2,1)S(1)} %get-tuple-element.60), channel_id=1, source_target_pairs={{1,2},{3,4},{5,6},{7,8},{9,10},{11,12},{13,14},{15,16},{17,18},{19... | collective-permute-start | bytes 6152 | tf_op jit(solution)/shard_map/ppermute | solution.py:409
  10.1 4.5 %collective-permute-start.2 = (bf16[8,128]{1,0:T(8,128)(2,1)S(1)}, bf16[8,128]{1,0:T(8,128)(2,1)S(1)}, u32[]{:S(2)}, u32[]{:S(2)}) collective-permute-start(bf16[8,128]{1,0:T(8,128)(2,1)S(1)} %get-tuple-element.62), channel_id=1, source_target_pairs={{0,1},{1,0},{2,3},{3,2},{4,5},{5,4},{6,7},{7,6},{8,9},{9,8},{10,11... | collective-permute-start | bytes 6152 | tf_op jit(solution)/shard_map/ppermute | solution.py:397

commit v8 on v7

--- a/solution.py
+++ b/solution.py
@@ -149,7 +149,8 @@
 
 def stage():
     slab = lax.axis_index("space")
-    return jnp.where(slab == 1, FIRST, jnp.where(slab == 0, EARLY, LATE))
+    first = jnp.logical_and(slab == 1, lax.axis_index("mode") > 0)
+    return jnp.where(first, FIRST, jnp.where(slab <= 1, EARLY, LATE))
 
 
 def early_kernel(state_ref, table_ref, thermal_ref, target_ref, tensor_hbm, coarse_ref, *refs):

time: 15.6 us -> 15.6 us (level)
  starting transfers between devices: 6.9 us -> 7.5 us
  waiting for transfers between devices: 1.22 us -> 0.65 us
    ppermute x1, waiting for transfers between devices: 1.22 us -> 0.61 us  [shards(): lax.ppermute(edge, ('space', 'mode'), pairs + [(j, i) for i, j in pairs])]
    ppermute x2, starting transfers between devices: 5.37 us -> 5.98 us  [shift(): lax.ppermute(x, 'mode', [(i, (i + by) % group) for i in range(group)])]
where the time goes in v8:
time: 15.6 us; the launch traced here: 15.4 us
  starting transfers between devices  7.5 us (48%)
  Pallas kernels  6.6 us (42%)
  between operations  0.68 us (4%)
  waiting for transfers between devices  0.65 us (4%)
    ppermute x2, starting transfers between devices, shift(): lax.ppermute(x, 'mode', [(i, (i + by) % group) for i in range(group)])  5.98 us
    pallas_call x2, Pallas kernels, preparing(): pl.pallas_call(kernel, in_specs=[VMEM, VMEM, SMEM, SMEM, HBM] + [VMEM] *...  2.38 us
    ppermute x1, starting transfers between devices, shards(): lax.ppermute(edge, ('space', 'mode'), pairs + [(j, i) for i, j in pairs])  1.52 us
    pallas_call x1, Pallas kernels, collide(): pl.pallas_call(collide_kernel, in_specs=[VMEM] * (3 + sets), out_shape=tu...  1.39 us
    pallas_call x1, Pallas kernels, coarsen(): pl.pallas_call(coarsen_kernel, in_specs=[HBM] * 5, out_shape=shapes + hel...  1.13 us
    pallas_call x1, Pallas kernels, place(): pl.pallas_call(place_kernel, in_specs=[SMEM, VMEM] + [VMEM] * (len(arrive...  0.8 us
    pallas_call x1, Pallas kernels, ends(): pl.pallas_call(ends_kernel, in_specs=[SMEM] + [VMEM] * 5, out_shape=pltpu...  0.75 us
    ppermute x1, waiting for transfers between devices, shards(): lax.ppermute(edge, ('space', 'mode'), pairs + [(j, i) for i, j in pairs])  0.61 us
  transfers between devices with their start and end apart: 3, of which 1 were waited for; matrix products, arithmetic and copies ran while one was open for 0% of the time, Pallas kernels for 30%

profile of v8, /device:TPU:0, one launch (start us, length us, event | category | flops | bytes accessed | tf_op | source)
XLA Modules:
  0.0 15.4 jit_solution(14612179381487939877)
XLA Ops:
  0.6 1.1 %coarsen.1 = (bf16[858,128]{1,0:T(8,128)(2,1)S(1)}, f32[858,128]{1,0:T(8,128)S(1)}, s32[3,286]{1,0:T(4,128)S(1)}, f32[3]{0:T(128)S(4)}, s32[16]{0:T(128)S(4)}, /...) custom-call(f32[858,128]{1,0:T(8,128)} %state_hbm.1, ...), custom_call_target="tpu_custom_call" | custom-call | tf_op jit(solution)/shard_map/coarsen/pallas_call | solution.py:79
  1.8 3.0 %collective-permute-start = (bf16[858,128]{1,0:T(8,128)(2,1)S(1)}, bf16[858,128]{1,0:T(8,128)(2,1)S(1)}, u32[]{:S(2)}, u32[]{:S(2)}) collective-permute-start(bf16[858,128]{1,0:T(8,128)(2,1)S(1)} %get-tuple-element.38.coarse_ref.refs_0_), channel_id=1, source_target_pairs={{0,1},{1,0},{2,3},{3,2},{4,5},{5,4},{6,7},{7,6},{8,9},{9,8},{10,11... | collective-permute-start | bytes 658952 | tf_op jit(solution)/shard_map/ppermute | solution.py:398
  4.8 2.4 %early_kernel.1 = (bf16[8,128]{1,0:T(8,128)(2,1)S(1)}, bf16[2288,858]{1,0:T(8,128)(2,1)S(1)}, bf16[286,286]{1,0:T(8,128)(2,1)S(1)}, bf16[286,286]{1,0:T(8,128)(2...) custom-call(f32[858,128]{1,0:T(8,128)S(1)} %get-tuple-element.36.sta, ...), custom_call_target="tpu_custom_call", output_to_operand_aliasing={{1}: (6, {}), {2}: (7, {}), {3}: (8, {}), {4}: (9, {}), {5}... | custom-call | tf_op jit(solution)/shard_map/early_kernel/pallas_call | solution.py:197
  7.2 1.5 %collective-permute-start.1 = (bf16[8,128]{1,0:T(8,128)(2,1)S(1)}, bf16[8,128]{1,0:T(8,128)(2,1)S(1)}, u32[]{:S(2)}, u32[]{:S(2)}) collective-permute-start(bf16[8,128]{1,0:T(8,128)(2,1)S(1)} %get-tuple-element.60), channel_id=1, source_target_pairs={{1,2},{3,4},{5,6},{7,8},{9,10},{11,12},{13,14},{15,16},{17,18},{19... | collective-permute-start | bytes 6152 | tf_op jit(solution)/shard_map/ppermute | solution.py:410
  8.7 0.0 collective-permute-done.refs_1_.left_ref.right_ref
  8.7 1.4 %collide.1 = (f32[8,128]{1,0:T(8,128)S(1)}, f32[8,128]{1,0:T(8,128)S(1)}, bf16[8,128]{1,0:T(8,128)(2,1)S(1)}) custom-call(bf16[2288,858]{1,0:T(8,128)(2,1)S(1)} %get-tuple-element.52.tensor_ref, s32[8,256]{1,0:T(8,128)S(1)} %get-tuple-element.53.kind_ref, f32[858,128]{1,0:T(8,128)S(1)} %get-tuple-element.54.own_ref, ...), custom_call_target="tpu_custom_call" | custom-call | tf_op jit(solution)/shard_map/collide/pallas_call | solution.py:264
  10.1 3.0 %collective-permute-start.2 = (bf16[8,128]{1,0:T(8,128)(2,1)S(1)}, bf16[8,128]{1,0:T(8,128)(2,1)S(1)}, u32[]{:S(2)}, u32[]{:S(2)}) collective-permute-start(bf16[8,128]{1,0:T(8,128)(2,1)S(1)} %get-tuple-element.62), channel_id=1, source_target_pairs={{0,1},{1,0},{2,3},{3,2},{4,5},{5,4},{6,7},{7,6},{8,9},{9,8},{10,11... | collective-permute-start | bytes 6152 | tf_op jit(solution)/shard_map/ppermute | solution.py:398
  13.1 0.2 %own_ends.1 = (f32[858,128]{1,0:T(8,128)S(1)}, f32[8,256]{1,0:T(8,128)S(1)}, f32[8,858]{1,0:T(8,128)S(1)}) custom-call(s32[16]{0:T(128)S(4)} %get-tuple-element.34.target_ref, f32[858,128]{1,0:T(8,128)S(1)} %get-tuple-element.51.inner_ref, bf16[858,128]{1,0:T(8,128)(2,1)S(1)} %collective-permute-done.refs_1_.left_ref.right_ref, ...), custom_call_target="tpu_custom_call", output_to_operand_aliasing={{0}: (1, {})} | custom-call | tf_op jit(solution)/shard_map/own_ends/pallas_call | solution.py:300
  13.2 0.6 %collective-permute-done.1.ring_ref = bf16[8,128]{1,0:T(8,128)(2,1)S(1)} collective-permute-done((bf16[8,128]{1,0:T(8,128)(2,1)S(1)}, bf16[8,128]{1,0:T(8,128)(2,1)S(1)}, u32[]{:S(2)}, u32[]{:S(2)}) %collective-permute-start.1) | collective-permute-done | bytes 2080 | tf_op jit(solution)/shard_map/ppermute | solution.py:410
  13.8 0.7 %ends.1._ = f32[858,128]{1,0:T(8,128)S(1)} custom-call(f32[3]{0:T(128)S(4)} %get-tuple-element.35.thermal_ref, f32[858,128]{1,0:T(8,128)S(1)} %get-tuple-element.57.inner_ref, bf16[286,286]{1,0:T(8,128)(2,1)S(1)} %get-tuple-element.58.high_ref, bf16[286,286]{1,0:T(8,128)(2,1)S(1)} %get-tuple-element.59.low_ref, ...), custom_call_target="tpu_custom_call", output_to_operand_aliasing={{}: (1, {})} | custom-call | tf_op jit(solution)/shard_map/ends/pallas_call | solution.py:346
  14.6 0.0 collective-permute-done.2.refs_0_
  14.6 0.8 %place.1 = (f32[858,128]{1,0:T(8,128)S(1)}, f32[858,128]{1,0:T(8,128)}, f32[8,256]{1,0:T(8,128)}) custom-call(s32[16]{0:T(128)S(4)} %get-tuple-element.34.target_ref, f32[858,128]{1,0:T(8,128)S(1)} %ends.1._, bf16[8,128]{1,0:T(8,128)(2,1)S(1)} %collective-permute-done.2.refs_0_, f32[8,256]{1,0:T(8,128)S(1)} %get-tuple-element.63.refs_1_), custom_call_target="tpu_custom_call", output_to_operand_aliasing={{0}: (1, {})} | custom-call | tf_op jit(solution)/shard_map/place/pallas_call | solution.py:376
  (1 shorter events, 0.0 us)
Async XLA Ops:
  1.8 7.0 %collective-permute-start = (bf16[858,128]{1,0:T(8,128)(2,1)S(1)}, bf16[858,128]{1,0:T(8,128)(2,1)S(1)}, u32[]{:S(2)}, u32[]{:S(2)}) collective-permute-start(bf16[858,128]{1,0:T(8,128)(2,1)S(1)} %get-tuple-element.38.coarse_ref.refs_0_), channel_id=1, source_target_pairs={{0,1},{1,0},{2,3},{3,2},{4,5},{5,4},{6,7},{7,6},{8,9},{9,8},{10,11... | collective-permute-start | bytes 658952 | tf_op jit(solution)/shard_map/ppermute | solution.py:398
  7.2 6.7 %collective-permute-start.1 = (bf16[8,128]{1,0:T(8,128)(2,1)S(1)}, bf16[8,128]{1,0:T(8,128)(2,1)S(1)}, u32[]{:S(2)}, u32[]{:S(2)}) collective-permute-start(bf16[8,128]{1,0:T(8,128)(2,1)S(1)} %get-tuple-element.60), channel_id=1, source_target_pairs={{1,2},{3,4},{5,6},{7,8},{9,10},{11,12},{13,14},{15,16},{17,18},{19... | collective-permute-start | bytes 6152 | tf_op jit(solution)/shard_map/ppermute | solution.py:410
  10.1 4.5 %collective-permute-start.2 = (bf16[8,128]{1,0:T(8,128)(2,1)S(1)}, bf16[8,128]{1,0:T(8,128)(2,1)S(1)}, u32[]{:S(2)}, u32[]{:S(2)}) collective-permute-start(bf16[8,128]{1,0:T(8,128)(2,1)S(1)} %get-tuple-element.62), channel_id=1, source_target_pairs={{0,1},{1,0},{2,3},{3,2},{4,5},{5,4},{6,7},{7,6},{8,9},{9,8},{10,11... | collective-permute-start | bytes 6152 | tf_op jit(solution)/shard_map/ppermute | solution.py:398
